TPU v7x, 32 devices: a whole 2x2x4 slice. The times are simulated.
32 devices in a mesh: dp: 8 (over z, y), tensor: 4 (over x, core).
Axes of the slice: x: 2, y: 2, z: 4, core: 2. Of those that a mesh axis runs over, the one named last changes fastest.
Arguments:
- tokens: bfloat16 [16384, 1024], P('dp', 'tensor'), may hold values from -6 to 6
- lengths: int32 [8, 6], P('dp'), may hold values from 0 to 1024, as said below
- gain_one: bfloat16 [1024], P('tensor'), may hold values from 0.5 to 1.5
- weight_in: bfloat16 [3, 1024, 1024], P(None, None, 'tensor'), may hold values from -0.1875 to 0.1875
- conv_taps: bfloat16 [3, 1024], P(None, 'tensor'), may hold values from -1 to 1
- weight_out: bfloat16 [1024, 1024], P('tensor'), may hold values from -0.1875 to 0.1875
- gain_two: bfloat16 [1024], P('tensor'), may hold values from 0.5 to 1.5
- weight_feed: bfloat16 [2, 1024, 4608], P(None, None, 'tensor'), may hold values from -0.1875 to 0.1875
- weight_down: bfloat16 [4608, 1024], P('tensor'), may hold values from -0.09375 to 0.09375
- grad_out: bfloat16 [16384, 1024], P('dp', 'tensor'), may hold values from -6 to 6
Outputs:
- block_out: bfloat16 [16384, 1024], P('dp', 'tensor')
- grad_tokens: bfloat16 [16384, 1024], P('dp', 'tensor')
- grad_gain_one: float32 [1024], P('tensor')
- grad_weight_in: float32 [3, 1024, 1024], P(None, 'dp', 'tensor')
- grad_conv_taps: float32 [3, 1024], P(None, 'tensor')
- grad_weight_out: float32 [1024, 1024], P('tensor', 'dp')
- grad_gain_two: float32 [1024], P('tensor')
- grad_weight_feed: float32 [2, 1024, 4608], P(None, 'dp', 'tensor')
- grad_weight_down: float32 [4608, 1024], P('tensor', 'dp')
Inputs may be any that keep to these rules, and one draw needn't show every extreme that they name: `lengths`: row g lists the documents of the slots of index g of dp in order, zeros being empty slots; each row sums to at most 2048, some row to exactly 2048, and some document has exactly 1024 tokens.
All inputs are finite; a program needn't handle non-finite values.
Results may differ from a plain program's by a relative error of at most 0.0091.
Values may be sent and summed in bfloat16 or wider, within the bound.
A program may use at most 192 MiB of HBM per device.

v0:
```python
import jax
import jax.numpy as jnp
from jax import lax
from jax.sharding import PartitionSpec as P

EPSILON = 1e-05


def shift_down(values, offset):
    return jnp.concatenate(
        [jnp.zeros((offset,) + values.shape[1:], values.dtype), values[:-offset]], axis=0
    )


def shift_up(values, offset):
    return jnp.concatenate(
        [values[offset:], jnp.zeros((offset,) + values.shape[1:], values.dtype)], axis=0
    )


def body(
    tokens,
    lengths,
    gain_one,
    weight_in,
    conv_taps,
    weight_out,
    gain_two,
    weight_feed,
    weight_down,
    grad_out,
):
    row_count = tokens.shape[0]
    part_width = tokens.shape[1]
    full_width = part_width * lax.axis_size("tensor")
    feed_width = weight_feed.shape[2]
    column_start = lax.axis_index("tensor") * part_width
    doc_ends = jnp.cumsum(lengths[0])
    live_count = doc_ends[-1]
    positions = jnp.arange(row_count, dtype=jnp.int32)
    segments = jnp.sum((positions[:, None] >= doc_ends[None, :]).astype(jnp.int32), axis=1)
    live_mask = (positions < live_count).astype(jnp.float32)[:, None]
    same_one = jnp.concatenate(
        [jnp.zeros((1,), jnp.float32), (segments[1:] == segments[:-1]).astype(jnp.float32)]
    )[:, None]
    same_two = jnp.concatenate(
        [jnp.zeros((2,), jnp.float32), (segments[2:] == segments[:-2]).astype(jnp.float32)]
    )[:, None]
    block_rows = min(512, row_count)
    loop_count = (live_count + block_rows - 1) // block_rows
    gathered, gain_full = (
        lax.all_gather(tokens, "tensor", axis=1, tiled=True),
        lax.all_gather(gain_one, "tensor", axis=0, tiled=True),
    )
    tokens_full = gathered.astype(jnp.float32)
    scale_one = lax.rsqrt(jnp.mean(tokens_full * tokens_full, axis=1, keepdims=True) + EPSILON)
    unit_one = tokens_full * scale_one
    normed_one = (unit_one * gain_full.astype(jnp.float32)).astype(jnp.bfloat16)
    gate_block = jnp.einsum(
        "td,gde->gte", normed_one, weight_in, preferred_element_type=jnp.float32
    )
    gate_b = gate_block[0]
    gate_c = gate_block[1]
    gate_x = gate_block[2]
    mixed_in = gate_b * gate_x
    prev_one = shift_down(mixed_in, 1) * same_one
    prev_two = shift_down(mixed_in, 2) * same_two
    taps_f = conv_taps.astype(jnp.float32)
    conv_out = taps_f[2] * mixed_in + taps_f[1] * prev_one + taps_f[0] * prev_two
    mixer_rows = (gate_c * conv_out).astype(jnp.bfloat16)
    mixer_part = jnp.dot(mixer_rows, weight_out, preferred_element_type=jnp.float32)
    mixer_out = lax.psum_scatter(mixer_part, "tensor", scatter_dimension=1, tiled=True)
    middle = tokens.astype(jnp.float32) + live_mask * mixer_out
    square_sum = lax.psum(jnp.sum(middle * middle, axis=1), "tensor")
    scale_two = lax.rsqrt(square_sum / full_width + EPSILON)[:, None]
    unit_two = middle * scale_two
    gain_two_f = gain_two.astype(jnp.float32)
    normed_part = (unit_two * gain_two_f).astype(jnp.bfloat16)
    normed_two = lax.all_gather(normed_part, "tensor", axis=1, tiled=True)

    def feed_forward_step(step_index, state_tuple):
        kept_gu, kept_hidden, feed_part = state_tuple
        start = step_index * block_rows
        normed_rows = lax.dynamic_slice_in_dim(normed_two, start, block_rows, 0)
        gate_up = jnp.einsum(
            "td,kdf->ktf", normed_rows, weight_feed, preferred_element_type=jnp.float32
        )
        hidden = (jax.nn.silu(gate_up[0]) * gate_up[1]).astype(jnp.bfloat16)
        feed_rows = jnp.dot(hidden, weight_down, preferred_element_type=jnp.float32)
        kept_gu = lax.dynamic_update_slice_in_dim(kept_gu, gate_up, start, 1)
        kept_hidden = lax.dynamic_update_slice_in_dim(kept_hidden, hidden, start, 0)
        feed_part = lax.dynamic_update_slice_in_dim(feed_part, feed_rows, start, 0)
        return (kept_gu, kept_hidden, feed_part)

    first_state = (
        jnp.zeros((2, row_count, feed_width), jnp.float32),
        jnp.zeros((row_count, feed_width), jnp.bfloat16),
        jnp.zeros((row_count, full_width), jnp.float32),
    )
    kept_gu, kept_hidden, feed_part = lax.fori_loop(0, loop_count, feed_forward_step, first_state)
    feed_out = lax.psum_scatter(
        feed_part.astype(jnp.bfloat16), "tensor", scatter_dimension=1, tiled=True
    ).astype(jnp.float32)
    block_out = (middle + live_mask * feed_out).astype(jnp.bfloat16)
    grad_full = lax.all_gather(grad_out, "tensor", axis=1, tiled=True)
    feed_grad = jnp.where(live_mask > 0.0, grad_full, jnp.zeros_like(grad_full))

    def feed_backward_step(step_index, state_tuple):
        grad_feed, grad_down, normed_grad = state_tuple
        start = step_index * block_rows
        grad_rows = lax.dynamic_slice_in_dim(feed_grad, start, block_rows, 0)
        gate_up = lax.dynamic_slice_in_dim(kept_gu, start, block_rows, 1)
        hidden = lax.dynamic_slice_in_dim(kept_hidden, start, block_rows, 0)
        normed_rows = lax.dynamic_slice_in_dim(normed_two, start, block_rows, 0)
        hidden_grad = lax.dot_general(
            grad_rows, weight_down, (((1,), (1,)), ((), ())), preferred_element_type=jnp.float32
        )
        gate_vals = gate_up[0]
        up_vals = gate_up[1]
        sigmoid_vals = jax.nn.sigmoid(gate_vals)
        gate_grad = hidden_grad * up_vals * sigmoid_vals * (1.0 + gate_vals * (1.0 - sigmoid_vals))
        up_grad = hidden_grad * (gate_vals * sigmoid_vals)
        gu_grad = jnp.stack([gate_grad, up_grad]).astype(jnp.bfloat16)
        grad_down = grad_down + lax.dot_general(
            hidden, grad_rows, (((0,), (0,)), ((), ())), preferred_element_type=jnp.float32
        )
        grad_feed = grad_feed + jnp.einsum(
            "td,ktf->kdf", normed_rows, gu_grad, preferred_element_type=jnp.float32
        )
        row_grad = jnp.einsum(
            "ktf,kdf->td", gu_grad, weight_feed, preferred_element_type=jnp.float32
        )
        normed_grad = lax.dynamic_update_slice_in_dim(normed_grad, row_grad, start, 0)
        return (grad_feed, grad_down, normed_grad)

    back_state = (
        jnp.zeros((2, full_width, feed_width), jnp.float32),
        jnp.zeros((feed_width, full_width), jnp.float32),
        jnp.zeros((row_count, full_width), jnp.float32),
    )
    grad_feed, grad_down, normed_grad = lax.fori_loop(0, loop_count, feed_backward_step, back_state)
    normed_two_grad = lax.psum_scatter(normed_grad, "tensor", scatter_dimension=1, tiled=True)
    grad_gain_two = jnp.sum(normed_two_grad * unit_two, axis=0)
    scaled_two = normed_two_grad * gain_two_f
    inner_two = lax.psum(jnp.sum(scaled_two * unit_two, axis=1), "tensor")
    middle_grad = grad_out.astype(jnp.float32) + scale_two * (
        scaled_two - unit_two * (inner_two / full_width)[:, None]
    )
    mixer_grad_part = (middle_grad * live_mask).astype(jnp.bfloat16)
    mixer_grad = lax.all_gather(mixer_grad_part, "tensor", axis=1, tiled=True)
    grad_out_weight = lax.dot_general(
        mixer_rows, mixer_grad, (((0,), (0,)), ((), ())), preferred_element_type=jnp.float32
    )
    rows_grad = lax.dot_general(
        mixer_grad, weight_out, (((1,), (1,)), ((), ())), preferred_element_type=jnp.float32
    )
    c_grad = rows_grad * conv_out
    conv_grad = rows_grad * gate_c
    grad_taps = jnp.stack(
        [
            jnp.sum(conv_grad * prev_two, axis=0),
            jnp.sum(conv_grad * prev_one, axis=0),
            jnp.sum(conv_grad * mixed_in, axis=0),
        ]
    )
    mixed_grad = (
        taps_f[2] * conv_grad
        + taps_f[1] * shift_up(conv_grad * same_one, 1)
        + taps_f[0] * shift_up(conv_grad * same_two, 2)
    )
    gates_grad = jnp.stack([mixed_grad * gate_x, c_grad, mixed_grad * gate_b]).astype(jnp.bfloat16)
    grad_in_weight = jnp.einsum(
        "td,gte->gde", normed_one, gates_grad, preferred_element_type=jnp.float32
    )
    normed_one_part = jnp.einsum(
        "gte,gde->td", gates_grad, weight_in, preferred_element_type=jnp.float32
    )
    normed_one_grad = lax.psum_scatter(normed_one_part, "tensor", scatter_dimension=1, tiled=True)
    unit_part = lax.dynamic_slice_in_dim(unit_one, column_start, part_width, 1)
    grad_gain_one = jnp.sum(normed_one_grad * unit_part, axis=0)
    scaled_one = normed_one_grad * gain_one.astype(jnp.float32)
    inner_one = lax.psum(jnp.sum(scaled_one * unit_part, axis=1), "tensor")
    tokens_grad = middle_grad + scale_one * (
        scaled_one - unit_part * (inner_one / full_width)[:, None]
    )
    in_shard, out_shard, feed_shard, down_shard = (
        lax.psum_scatter(grad_in_weight, "dp", scatter_dimension=1, tiled=True),
        lax.psum_scatter(grad_out_weight, "dp", scatter_dimension=1, tiled=True),
        lax.psum_scatter(grad_feed, "dp", scatter_dimension=1, tiled=True),
        lax.psum_scatter(grad_down, "dp", scatter_dimension=1, tiled=True),
    )
    gain_one_sum, gain_two_sum, taps_sum = lax.psum((grad_gain_one, grad_gain_two, grad_taps), "dp")
    return (
        block_out,
        tokens_grad.astype(jnp.bfloat16),
        gain_one_sum,
        in_shard,
        taps_sum,
        out_shard,
        gain_two_sum,
        feed_shard,
        down_shard,
    )


def solution(mesh):
    placed = (
        P("dp", "tensor"),
        P("dp", None),
        P("tensor"),
        P(None, None, "tensor"),
        P(None, "tensor"),
        P("tensor", None),
        P("tensor"),
        P(None, None, "tensor"),
        P("tensor", None),
        P("dp", "tensor"),
    )
    return jax.shard_map(
        body,
        mesh=mesh,
        in_specs=placed,
        out_specs=(
            P("dp", "tensor"),
            P("dp", "tensor"),
            P("tensor"),
            P(None, "dp", "tensor"),
            P(None, "tensor"),
            P("tensor", "dp"),
            P("tensor"),
            P(None, "dp", "tensor"),
            P("tensor", "dp"),
        ),
        check_vma=False,
    )
```

profile of v0, /device:TPU:0, one launch (start us, length us, event | category | flops | bytes accessed | tf_op | source)
XLA Modules:
  0.0 1055.3 jit_solution(3777354400168406079)
XLA Ops:
  8.6 6.0 all-gather
  16.6 30.7 %all-gather.6.cloned.1.call-done = bf16[2048,1024]{1,0:T(8,128)(2,1)} async-done(((bf16[2048,256]{1,0:T(8,128)(2,1)}), bf16[2048,1024]{1,0:T(8,128)(2,1)}) %all-gather.6.cloned.1.call-update) | async-done | bytes 4194320 | tf_op jit(solution)/shard_map/all_gather | solution.py:52
  66.9 69.8 %reduce-scatter.9.cloned.1.call-done = f32[2048,256]{1,0:T(8,128)} async-done(((f32[2048,1024]{1,0:T(8,128)}), f32[2048,256]{1,0:T(8,128)}) %reduce-scatter.9.cloned.1.call-update) | async-done | bytes 2097168 | tf_op jit(solution)/shard_map/reduce_scatter | solution.py:72
  153.6 19.8 %all-gather.10.cloned.1.call-done = bf16[2048,1024]{1,0:T(8,128)(2,1)} async-done(((bf16[2048,256]{1,0:T(8,128)(2,1)}), bf16[2048,1024]{1,0:T(8,128)(2,1)}) %all-gather.10.cloned.1.call-update) | async-done | bytes 4194320 | tf_op jit(solution)/shard_map/all_gather | solution.py:105
  177.3 33.2 %all-gather.8.cloned.1.call-done = bf16[2048,1024]{1,0:T(8,128)(2,1)} async-done(((bf16[2048,256]{1,0:T(8,128)(2,1)}), bf16[2048,1024]{1,0:T(8,128)(2,1)}) %all-gather.8.cloned.1.call-update) | async-done | bytes 4194320 | tf_op jit(solution)/shard_map/all_gather | solution.py:79
  210.5 7.7 broadcast_in_dim.15
  220.6 43.0 %while.28 = (s32[]{:T(128)}, f32[2,2048,1152]{2,1,0:T(8,128)}, bf16[2048,1152]{1,0:T(8,128)(2,1)}, bf16[2048,1024]{1,0:T(8,128)(2,1)}, s32[]{:T(128)}, /*index=5...) while((s32[]{:T(128)}, f32[2,2048,1152]{2,1,0:T(8,128)}, ...), condition=%wide.region_7.8_spmd, body=%wide.region_6.7_spmd.sunk | while | flops 3627417600 | bytes 70911224 | solution.py:100
  220.8 7.4 constant_dynamic-update-slice_fusion.4
  235.1 7.4 constant_dynamic-update-slice_fusion.4
  249.4 7.4 constant_dynamic-update-slice_fusion.4
  275.7 72.9 %while.29 = (s32[]{:T(128)}, f32[2,1024,1152]{1,2,0:T(8,128)}, f32[1152,1024]{1,0:T(8,128)}, f32[2048,1024]{1,0:T(8,128)}, s32[]{:T(128)}, /*index=5*/bf16[2048,...) while((s32[]{:T(128)}, f32[2,1024,1152]{1,2,0:T(8,128)}, ...), condition=%wide.region_10.11_spmd, body=%wide.region_9.10_spmd.sunk | while | flops 7261323264 | bytes 72485616 | solution.py:141
  285.5 7.9 bitcast_add_fusion.2
  293.4 6.7 convolution_add_fusion.2
  309.7 7.9 bitcast_add_fusion.2
  317.6 6.7 convolution_add_fusion.2
  333.9 7.9 bitcast_add_fusion.2
  341.8 6.8 convolution_add_fusion.2
  349.3 109.7 %reduce-scatter.13.cloned.1.call-done = f32[2048,256]{1,0:T(8,128)} async-done(((f32[2048,1024]{1,0:T(8,128)}), f32[2048,256]{1,0:T(8,128)}) %reduce-scatter.13.cloned.1.call-update) | async-done | bytes 2097168 | tf_op jit(solution)/shard_map/reduce_scatter | solution.py:142
  461.9 5.9 psum.43
  467.8 38.0 %reduce-scatter.11.cloned.1.call-done = bf16[2048,256]{1,0:T(8,128)(2,1)} async-done(((bf16[2048,1024]{1,0:T(8,128)(2,1)}), bf16[2048,256]{1,0:T(8,128)(2,1)}) %reduce-scatter.11.cloned.1.call-update) | async-done | bytes 1048592 | tf_op jit(solution)/shard_map/reduce_scatter | solution.py:101
  510.0 35.0 %all-gather.12.cloned.1.call-done = bf16[2048,1024]{1,0:T(8,128)(2,1)} async-done(((bf16[2048,256]{1,0:T(8,128)(2,1)}), bf16[2048,1024]{1,0:T(8,128)(2,1)}) %all-gather.12.cloned.1.call-update) | async-done | bytes 4194320 | tf_op jit(solution)/shard_map/all_gather | solution.py:150
  545.0 7.3 multiply_reduce_fusion.3
  564.7 7.6 convolution_bitcast_fusion.1
  572.9 9.7 copy.29
  587.9 6.3 convert_multiply_fusion
  594.3 45.8 %reduce-scatter.17.cloned.1.call-done = f32[3,128,256]{1,2,0:T(8,128)} async-done(((f32[3,1024,256]{1,2,0:T(8,128)}), f32[3,128,256]{1,2,0:T(8,128)}) %reduce-scatter.17.cloned.1.call-update) | async-done | bytes 393232 | tf_op jit(solution)/shard_map/reduce_scatter | solution.py:187
  641.9 71.8 %reduce-scatter.15.cloned.1.call-done = f32[2048,256]{1,0:T(8,128)} async-done(((f32[2048,1024]{1,0:T(8,128)}), f32[2048,256]{1,0:T(8,128)}) %reduce-scatter.15.cloned.1.call-update) | async-done | bytes 2097168 | tf_op jit(solution)/shard_map/reduce_scatter | solution.py:178
  716.4 22.9 %all-reduce.5 = (f32[256]{0:T(256)}, f32[3,256]{1,0:T(4,128)}, f32[256]{0:T(256)}) all-reduce(f32[256]{0:T(256)S(1)} %get-tuple-element.147, f32[3,256]{1,0:T(4,128)S(1)} %pad_maximum_fusion.6, f32[256]{0:T(256)S(1)} %get-tuple-element.149), channel_id=1, replica_groups=mesh['dp'=8,'tensor'=4] {'dp'}, use_global_device_ids=true, to_apply=%region_18.19 | all-reduce | flops 1280 | bytes 10240 | tf_op jit(solution)/shard_map/psum | solution.py:192
  739.4 6.1 psum.44
  750.6 63.2 %reduce-scatter.23.cloned.1.call-done = f32[1152,128]{1,0:T(8,128)} async-done(((f32[1152,1024]{1,0:T(8,128)}), f32[1152,128]{1,0:T(8,128)}) %reduce-scatter.23.cloned.1.call-update) | async-done | bytes 589840 | tf_op jit(solution)/shard_map/reduce_scatter | solution.py:190
  813.8 167.4 %reduce-scatter.21.cloned.1.call-done = f32[2,128,1152]{2,1,0:T(8,128)} async-done(((f32[2,1024,1152]{2,1,0:T(8,128)}), f32[2,128,1152]{2,1,0:T(8,128)}) %reduce-scatter.21.cloned.1.call-update) | async-done | bytes 1179664 | tf_op jit(solution)/shard_map/reduce_scatter | solution.py:189
  981.2 66.8 %reduce-scatter.19.cloned.1.call-done = f32[256,128]{1,0:T(8,128)} async-done(((f32[256,1024]{1,0:T(8,128)}), f32[256,128]{1,0:T(8,128)}) %reduce-scatter.19.cloned.1.call-update) | async-done | bytes 131088 | tf_op jit(solution)/shard_map/reduce_scatter | solution.py:188
  (175 shorter events, 142.4 us)
Async XLA Ops:
  7.2 43.4 %copy-start = (bf16[3,1024,256]{2,1,0:T(8,128)(2,1)S(1)}, bf16[3,1024,256]{2,1,0:T(8,128)(2,1)}, u32[]{:S(2)}) copy-start(bf16[3,1024,256]{2,1,0:T(8,128)(2,1)} %param.17) | copy-start | bytes 4718596
  7.2 40.1 %all-gather.6.cloned.1.call-start = ((), (), s32[]{:S(2)}) async-start(), calls=%async_computation.8 | async-start | bytes 5242880 | tf_op jit(solution)/shard_map/all_gather | solution.py:52
  7.9 128.8 %reduce-scatter.9.cloned.1.call-start = ((), (), s32[]{:S(2)}) async-start(), calls=%async_computation.9 | async-start | bytes 10485760 | tf_op jit(solution)/shard_map/reduce_scatter | solution.py:72
  14.6 39.7 %copy-start.33 = (f32[4,1,256]{2,1,0:T(1,128)}, f32[4,1,256]{2,1,0:T(1,128)S(1)}, u32[]{:S(2)}) copy-start(f32[4,1,256]{2,1,0:T(1,128)S(1)} %convert_element_type.82) | copy-start | bytes 12292
  15.8 38.8 %copy-start.17 = (f32[2048]{0:T(1024)}, f32[2048]{0:T(1024)S(1)}, u32[]{:S(2)}) copy-start(f32[2048]{0:T(1024)S(1)} %get-tuple-element.214) | copy-start | bytes 24580
  15.8 38.8 %copy-start.19 = (f32[2048]{0:T(1024)}, f32[2048]{0:T(1024)S(1)}, u32[]{:S(2)}) copy-start(f32[2048]{0:T(1024)S(1)} %get-tuple-element.215) | copy-start | bytes 24580
  16.6 38.1 %copy-start.27 = (f32[1,256]{1,0:T(1,128)}, f32[1,256]{1,0:T(1,128)S(1)}, u32[]{:S(2)}) copy-start(f32[1,256]{1,0:T(1,128)S(1)} %get-tuple-element.211) | copy-start | bytes 3076
  16.6 38.1 %copy-start.29 = (f32[1,256]{1,0:T(1,128)}, f32[1,256]{1,0:T(1,128)S(1)}, u32[]{:S(2)}) copy-start(f32[1,256]{1,0:T(1,128)S(1)} %get-tuple-element.212) | copy-start | bytes 3076
  16.6 38.1 %copy-start.31 = (f32[1,256]{1,0:T(1,128)}, f32[1,256]{1,0:T(1,128)S(1)}, u32[]{:S(2)}) copy-start(f32[1,256]{1,0:T(1,128)S(1)} %get-tuple-element.213) | copy-start | bytes 3076
  64.8 71.9 %copy-start.9 = (bf16[2048,256]{1,0:T(8,128)(2,1)S(1)}, bf16[2048,256]{1,0:T(8,128)(2,1)}, u32[]{:S(2)}) copy-start(bf16[2048,256]{1,0:T(8,128)(2,1)} %param.14) | copy-start | bytes 3145732
  64.8 108.6 %all-gather.10.cloned.1.call-start = ((), (), s32[]{:S(2)}) async-start(), calls=%async_computation.12 | async-start | bytes 5242880 | tf_op jit(solution)/shard_map/all_gather | solution.py:105
  65.6 145.0 %all-gather.8.cloned.1.call-start = ((), (), s32[]{:S(2)}) async-start(), calls=%async_computation.10 | async-start | bytes 5242880 | tf_op jit(solution)/shard_map/all_gather | solution.py:79
  66.2 79.7 %copy-start.25 = (f32[256]{0:T(256)}, f32[256]{0:T(256)S(1)}, u32[]{:S(2)}) copy-start(f32[256]{0:T(256)S(1)} %convert_element_type.73) | copy-start | bytes 3076
  66.9 73.1 %copy-start.21 = (f32[2048]{0:T(1024)}, f32[2048]{0:T(1024)S(1)}, u32[]{:S(2)}) copy-start(f32[2048]{0:T(1024)S(1)} %fusion.31) | copy-start | bytes 24580
  149.7 309.2 %reduce-scatter.13.cloned.1.call-start = ((), (), s32[]{:S(2)}) async-start(), calls=%async_computation.13 | async-start | bytes 10485760 | tf_op jit(solution)/shard_map/reduce_scatter | solution.py:142
  300.1 5.7 copy-start.35
  324.3 5.7 copy-start.35
  348.6 110.3 %copy-start.16 = (f32[2048]{0:T(1024)S(1)}, f32[2048]{0:T(1024)}, u32[]{:S(2)}) copy-start(f32[2048]{0:T(1024)} %copy-done.15) | copy-start | bytes 24580
  348.6 110.3 %copy-start.26 = (f32[256]{0:T(256)S(1)}, f32[256]{0:T(256)}, u32[]{:S(2)}) copy-start(f32[256]{0:T(256)} %copy-done.25) | copy-start | bytes 3076
  348.6 157.3 %reduce-scatter.11.cloned.1.call-start = ((), (), s32[]{:S(2)}) async-start(), calls=%async_computation.11 | async-start | bytes 5242880 | tf_op jit(solution)/shard_map/reduce_scatter | solution.py:101
  349.2 156.7 %copy-start.7 = (bf16[2048,256]{1,0:T(8,128)(2,1)S(1)}, bf16[2048,256]{1,0:T(8,128)(2,1)}, u32[]{:S(2)}) copy-start(bf16[2048,256]{1,0:T(8,128)(2,1)} %param.23) | copy-start | bytes 3145732
  349.2 156.7 %copy-start.22 = (f32[2048]{0:T(1024)S(1)}, f32[2048]{0:T(1024)}, u32[]{:S(2)}) copy-start(f32[2048]{0:T(1024)} %copy-done.21) | copy-start | bytes 24580
  349.2 195.8 %all-gather.12.cloned.1.call-start = ((), (), s32[]{:S(2)}) async-start(), calls=%async_computation.14 | async-start | bytes 5242880 | tf_op jit(solution)/shard_map/all_gather | solution.py:150
  467.8 42.1 %copy-start.18 = (f32[2048]{0:T(1024)S(1)}, f32[2048]{0:T(1024)}, u32[]{:S(2)}) copy-start(f32[2048]{0:T(1024)} %copy-done.17) | copy-start | bytes 24580
  467.8 42.2 %copy-start.20 = (f32[2048]{0:T(1024)S(1)}, f32[2048]{0:T(1024)}, u32[]{:S(2)}) copy-start(f32[2048]{0:T(1024)} %copy-done.19) | copy-start | bytes 24580
  467.8 77.2 %copy-start.11 = (bf16[256,1024]{1,0:T(8,128)(2,1)S(1)}, bf16[256,1024]{1,0:T(8,128)(2,1)}, u32[]{:S(2)}) copy-start(bf16[256,1024]{1,0:T(8,128)(2,1)} %param.19) | copy-start | bytes 1572868
  509.8 130.2 %reduce-scatter.17.cloned.1.call-start = ((), (), s32[]{:S(2)}) async-start(), calls=%async_computation.16 | async-start | bytes 3538944 | tf_op jit(solution)/shard_map/reduce_scatter | solution.py:187
  552.4 5.8 copy-start.12
  564.6 149.1 %reduce-scatter.15.cloned.1.call-start = ((), (), s32[]{:S(2)}) async-start(), calls=%async_computation.15 | async-start | bytes 10485760 | tf_op jit(solution)/shard_map/reduce_scatter | solution.py:178
  572.3 241.5 %reduce-scatter.23.cloned.1.call-start = ((), (), s32[]{:S(2)}) async-start(), calls=%async_computation.19 | async-start | bytes 5308416 | tf_op jit(solution)/shard_map/reduce_scatter | solution.py:190
  572.9 408.3 %reduce-scatter.21.cloned.1.call-start = ((), (), s32[]{:S(2)}) async-start(), calls=%async_computation.18 | async-start | bytes 10616832 | tf_op jit(solution)/shard_map/reduce_scatter | solution.py:189
  582.7 465.3 %reduce-scatter.19.cloned.1.call-start = ((), (), s32[]{:S(2)}) async-start(), calls=%async_computation.17 | async-start | bytes 1179648 | tf_op jit(solution)/shard_map/reduce_scatter | solution.py:188
  (27 other events, 70.7 us)
Sparse Core Ops, SparseCore 0:
  9.6 37.7 all-gather.5
  64.9 71.7 reduce-scatter.8
  138.3 35.0 all-gather.9
  175.5 35.0 all-gather.7
  348.7 110.1 reduce-scatter.12
  461.3 44.5 reduce-scatter.10
  510.0 35.0 all-gather.11
  564.8 75.2 reduce-scatter.16
  642.8 70.9 reduce-scatter.14
  717.8 95.9 reduce-scatter.22
  818.0 163.2 reduce-scatter.20
  985.1 62.9 reduce-scatter.18
where the time goes:
time: 1060 us
  waiting for transfers between devices  754 us (71%)
  matrix products  133 us (13%)
  other arithmetic  52.7 us (5%)
  local copies, waits for them, and re-layouts  52.5 us (5%)
  blocking collectives  46.7 us (4%)
  between operations  15.8 us (1%)
    reduce_scatter x1, waiting for transfers between devices, body(): lax.psum_scatter(grad_feed, 'dp', scatter_dimension=1, tiled=True)  167 us
    reduce_scatter x1, waiting for transfers between devices, body(): lax.psum_scatter(normed_grad, 'tensor', scatter_dimension=1, tiled=True)  110 us
    reduce_scatter x1, waiting for transfers between devices, body(): lax.psum_scatter(normed_one_part, 'tensor', scatter_dimension=1, tiled=True)  71.8 us
    reduce_scatter x1, waiting for transfers between devices, body(): lax.psum_scatter(mixer_part, 'tensor', scatter_dimension=1, tiled=True)  69.8 us
    reduce_scatter x1, waiting for transfers between devices, body(): lax.psum_scatter(grad_out_weight, 'dp', scatter_dimension=1, tiled=True)  66.8 us
    reduce_scatter x1, waiting for transfers between devices, body(): lax.psum_scatter(grad_down, 'dp', scatter_dimension=1, tiled=True)  63.2 us
    reduce_scatter x1, waiting for transfers between devices, body(): lax.psum_scatter(grad_in_weight, 'dp', scatter_dimension=1, tiled=True)  45.8 us
    reduce_scatter x1, waiting for transfers between devices, body(): lax.psum_scatter(feed_part.astype(jnp.bfloat16), 'tensor', scatter_dimens...  38 us
  transfers between devices with their start and end apart: 12, of which 12 were waited for; matrix products, arithmetic and copies ran while one was open for 6% of the time, Pallas kernels for 0%

commit v1 on v0

v1 whole, which is shorter than its diff:
```python
import jax
import jax.numpy as jnp
from jax import lax
from jax.sharding import PartitionSpec as P

EPSILON = 1e-05
CHUNKS = 2
F32 = jnp.float32
BF16 = jnp.bfloat16


def swap_core(values):
    size = lax.axis_size("tensor")
    return lax.ppermute(values, "tensor", [(i, i ^ 1) for i in range(size)])


def swap_chip(values):
    size = lax.axis_size("tensor")
    return lax.ppermute(values, "tensor", [(i, i ^ 2) for i in range(size)])


def ordered(is_first, own, other):
    return jnp.where(
        is_first,
        jnp.concatenate([own, other], axis=-1),
        jnp.concatenate([other, own], axis=-1),
    )


def gather_columns(values, core, chip):
    from_chip = swap_chip(values)
    from_core = swap_core(values)
    from_both = swap_core(from_chip)
    near = ordered(core == 0, values, from_core)
    far = ordered(core == 0, from_chip, from_both)
    return ordered(chip == 0, near, far)


def split_columns(weight, axis, core, chip):
    width = weight.shape[axis] // 4

    def block(chip_at, core_at):
        return lax.dynamic_slice_in_dim(weight, (chip_at * 2 + core_at) * width, width, axis)

    kept = jnp.concatenate([block(1 - chip, core), block(chip, core)], axis=axis)
    sent = jnp.concatenate([block(1 - chip, 1 - core), block(chip, 1 - core)], axis=axis)
    return sent, kept


def scatter_columns(sent, kept):
    total = kept + swap_core(sent.astype(BF16)).astype(F32)
    width = total.shape[1] // 2
    return total[:, width:] + swap_chip(total[:, :width].astype(BF16)).astype(F32)


def sum_tensor(values):
    values = values + swap_core(values)
    return values + swap_chip(values)


def sum_groups(values):
    size = lax.axis_size("dp")
    step = 1
    while step < size:
        values = values + lax.ppermute(values, "dp", [(i, i ^ step) for i in range(size)])
        step *= 2
    return values


def total_of(parts):
    result = parts[0]
    for part in parts[1:]:
        result = result + part
    return result


def dot_rows(left, right):
    return lax.dot_general(left, right, (((0,), (0,)), ((), ())), preferred_element_type=F32)


def dot_last(left, right):
    return lax.dot_general(left, right, (((1,), (1,)), ((), ())), preferred_element_type=F32)


def body(
    tokens,
    lengths,
    gain_one,
    weight_in,
    conv_taps,
    weight_out,
    gain_two,
    weight_feed,
    weight_down,
    grad_out,
):
    row_count = tokens.shape[0]
    part_width = tokens.shape[1]
    full_width = part_width * lax.axis_size("tensor")
    index = lax.axis_index("tensor")
    core, chip = index % 2, index // 2
    doc_ends = jnp.cumsum(lengths[0])
    positions = jnp.arange(row_count, dtype=jnp.int32)
    segments = jnp.sum((positions[:, None] >= doc_ends[None, :]).astype(jnp.int32), axis=1)
    live_all = (positions < doc_ends[-1]).astype(F32)[:, None]
    same_one_all = jnp.concatenate(
        [jnp.zeros((1,), F32), (segments[1:] == segments[:-1]).astype(F32)]
    )[:, None]
    same_two_all = jnp.concatenate(
        [jnp.zeros((2,), F32), (segments[2:] == segments[:-2]).astype(F32)]
    )[:, None]
    rows = row_count // CHUNKS

    def cut(array):
        return [array[k * rows : (k + 1) * rows] for k in range(CHUNKS)]

    live, same_one, same_two = cut(live_all), cut(same_one_all), cut(same_two_all)
    token_parts, grad_parts = cut(tokens), cut(grad_out)
    span = range(CHUNKS)

    gains = gather_columns(jnp.stack([gain_one, gain_two]), core, chip).astype(F32)
    gain_one_full, gain_two_full = gains[0:1], gains[1:2]
    token_full = [gather_columns(part, core, chip) for part in token_parts]
    held = lax.optimization_barrier(tuple(grad_parts) + tuple(token_full))
    grad_later, token_full = held[:CHUNKS], held[CHUNKS:]

    out_sent, out_kept = split_columns(weight_out, 1, core, chip)
    down_sent, down_kept = split_columns(weight_down, 1, core, chip)
    feed_sent, feed_kept = split_columns(weight_feed, 1, core, chip)
    in_sent, in_kept = split_columns(weight_in, 1, core, chip)
    taps = conv_taps.astype(F32)

    normed_one, gates, mixed, prev_one, prev_two, conv = [], [], [], [], [], []
    mixer_rows, middle, middle_full, scale_one = [], [], [], []
    for k in span:
        wide = token_full[k].astype(F32)
        scale = lax.rsqrt(jnp.mean(wide * wide, axis=1, keepdims=True) + EPSILON)
        scale_one.append(scale)
        normed_one.append((wide * scale * gain_one_full).astype(BF16))
        gate = jnp.einsum("td,gde->gte", normed_one[k], weight_in, preferred_element_type=F32)
        gates.append(gate)
        mix = gate[0] * gate[2]
        mixed.append(mix)
        before = mixed[k - 1][-2:] if k else jnp.zeros((2, part_width), F32)
        extended = jnp.concatenate([before, mix], axis=0)
        prev_one.append(extended[1:-1] * same_one[k])
        prev_two.append(extended[:-2] * same_two[k])
        conv.append(taps[2] * mix + taps[1] * prev_one[k] + taps[0] * prev_two[k])
        mixer_rows.append((gate[1] * conv[k]).astype(BF16))
        mixer_out = scatter_columns(
            jnp.dot(mixer_rows[k], out_sent, preferred_element_type=F32),
            jnp.dot(mixer_rows[k], out_kept, preferred_element_type=F32),
        )
        middle.append(token_parts[k].astype(F32) + live[k] * mixer_out)
        middle_full.append(gather_columns(middle[k].astype(BF16), core, chip))

    grad_full = [gather_columns(part, core, chip) for part in grad_later]
    normed_two, hidden, feed_grad, gu_grad, block_out = [], [], [], [], []
    middle_grad, mixer_grad, gain_two_parts = [], [], []
    for k in span:
        wide = middle_full[k].astype(F32)
        scale = lax.rsqrt(jnp.mean(wide * wide, axis=1, keepdims=True) + EPSILON)
        normed_two.append((wide * scale * gain_two_full).astype(BF16))
        gate_up = jnp.einsum("td,kdf->ktf", normed_two[k], weight_feed, preferred_element_type=F32)
        gate, up = gate_up[0], gate_up[1]
        sigmoid = jax.nn.sigmoid(gate)
        hidden.append((gate * sigmoid * up).astype(BF16))
        feed_grad.append(jnp.where(live[k] > 0.0, grad_full[k], jnp.zeros_like(grad_full[k])))
        hidden_grad = dot_last(feed_grad[k], weight_down)
        gate_grad = hidden_grad * up * sigmoid * (1.0 + gate * (1.0 - sigmoid))
        up_grad = hidden_grad * (gate * sigmoid)
        inner = sum_tensor(jnp.sum(gate_grad * gate + up_grad * up, axis=1))
        gu_grad.append(jnp.stack([gate_grad, up_grad]).astype(BF16))
        normed_grad = scatter_columns(
            jnp.einsum("ktf,kdf->td", gu_grad[k], feed_sent, preferred_element_type=F32),
            jnp.einsum("ktf,kdf->td", gu_grad[k], feed_kept, preferred_element_type=F32),
        )
        unit = middle[k] * scale
        gain_two_parts.append(jnp.sum(normed_grad * unit, axis=0))
        middle_grad.append(
            grad_parts[k].astype(F32)
            + scale
            * (normed_grad * gain_two.astype(F32) - unit * (inner / full_width)[:, None])
        )
        mixer_grad.append(gather_columns((middle_grad[k] * live[k]).astype(BF16), core, chip))
    grad_feed = total_of(
        [
            jnp.einsum("td,ktf->kdf", normed_two[k], gu_grad[k], preferred_element_type=F32)
            for k in span
        ]
    ).astype(BF16)
    feed_shard = lax.psum_scatter(grad_feed, "dp", scatter_dimension=1, tiled=True)
    grad_down = total_of([dot_rows(hidden[k], feed_grad[k]) for k in span]).astype(BF16)
    down_shard = lax.psum_scatter(grad_down, "dp", scatter_dimension=1, tiled=True)

    c_grad, conv_grad = [], []
    for k in span:
        rows_grad = dot_last(mixer_grad[k], weight_out)
        c_grad.append(rows_grad * conv[k])
        conv_grad.append(rows_grad * gates[k][1])
    grad_out_weight = total_of([dot_rows(mixer_rows[k], mixer_grad[k]) for k in span])
    out_shard = lax.psum_scatter(
        grad_out_weight.astype(BF16), "dp", scatter_dimension=1, tiled=True
    )
    grad_taps = jnp.stack(
        [
            total_of([jnp.sum(conv_grad[k] * prev_two[k], axis=0) for k in span]),
            total_of([jnp.sum(conv_grad[k] * prev_one[k], axis=0) for k in span]),
            total_of([jnp.sum(conv_grad[k] * mixed[k], axis=0) for k in span]),
        ]
    )
    gates_grad, gain_one_parts, tokens_grad = [], [], []
    for k in span:
        edge = jnp.zeros((2, part_width), F32)
        last = k == CHUNKS - 1
        after_one = edge if last else conv_grad[k + 1][:2] * same_one[k + 1][:2]
        after_two = edge if last else conv_grad[k + 1][:2] * same_two[k + 1][:2]
        next_one = jnp.concatenate([(conv_grad[k] * same_one[k])[1:], after_one[:1]], axis=0)
        next_two = jnp.concatenate([(conv_grad[k] * same_two[k])[2:], after_two], axis=0)
        mixed_grad = taps[2] * conv_grad[k] + taps[1] * next_one + taps[0] * next_two
        b_grad, x_grad = mixed_grad * gates[k][2], mixed_grad * gates[k][0]
        inner = sum_tensor(
            jnp.sum(b_grad * gates[k][0] + c_grad[k] * gates[k][1] + x_grad * gates[k][2], axis=1)
        )
        gates_grad.append(jnp.stack([b_grad, c_grad[k], x_grad]).astype(BF16))
        normed_grad = scatter_columns(
            jnp.einsum("gte,gde->td", gates_grad[k], in_sent, preferred_element_type=F32),
            jnp.einsum("gte,gde->td", gates_grad[k], in_kept, preferred_element_type=F32),
        )
        unit = token_parts[k].astype(F32) * scale_one[k]
        gain_one_parts.append(jnp.sum(normed_grad * unit, axis=0))
        tokens_grad.append(
            middle_grad[k]
            + scale_one[k]
            * (normed_grad * gain_one.astype(F32) - unit * (inner / full_width)[:, None])
        )
    grad_in_weight = total_of(
        [
            jnp.einsum("td,gte->gde", normed_one[k], gates_grad[k], preferred_element_type=F32)
            for k in span
        ]
    ).astype(BF16)
    in_shard = lax.psum_scatter(grad_in_weight, "dp", scatter_dimension=1, tiled=True)

    for k in span:
        feed_out = scatter_columns(
            jnp.dot(hidden[k], down_sent, preferred_element_type=F32),
            jnp.dot(hidden[k], down_kept, preferred_element_type=F32),
        )
        block_out.append((middle[k] + live[k] * feed_out).astype(BF16))

    small = sum_groups(jnp.concatenate([total_of(gain_two_parts)[None], grad_taps], axis=0))
    gain_one_sum = sum_groups(total_of(gain_one_parts))
    return (
        jnp.concatenate(block_out, axis=0),
        jnp.concatenate([part.astype(BF16) for part in tokens_grad], axis=0),
        gain_one_sum,
        in_shard.astype(F32),
        small[1:],
        out_shard.astype(F32),
        small[0],
        feed_shard.astype(F32),
        down_shard.astype(F32),
    )


def solution(mesh):
    placed = (
        P("dp", "tensor"),
        P("dp", None),
        P("tensor"),
        P(None, None, "tensor"),
        P(None, "tensor"),
        P("tensor", None),
        P("tensor"),
        P(None, None, "tensor"),
        P("tensor", None),
        P("dp", "tensor"),
    )
    return jax.shard_map(
        body,
        mesh=mesh,
        in_specs=placed,
        out_specs=(
            P("dp", "tensor"),
            P("dp", "tensor"),
            P("tensor"),
            P(None, "dp", "tensor"),
            P(None, "tensor"),
            P("tensor", "dp"),
            P("tensor"),
            P(None, "dp", "tensor"),
            P("tensor", "dp"),
        ),
        check_vma=False,
    )
```

time: 1060 us -> 622 us (0.59)
  waiting for transfers between devices: 754 us -> 340 us
  blocking collectives: 46.7 us -> 0 us
  starting transfers between devices: 0.95 us -> 36.7 us
  matrix products: 133 us -> 113 us
  local copies, waits for them, and re-layouts: 52.5 us -> 65.4 us
  other arithmetic: 52.7 us -> 41.1 us
    reduce_scatter x8 -> x0, waiting for transfers between devices: 633 us -> none  [the longest x1 167 us: body(): lax.psum_scatter(grad_feed, 'dp', scatter_dimension=1, tiled=True)]
    ppermute x0 -> x57, waiting for transfers between devices: none -> 169 us  [the longest x21 155 us: swap_chip(): return lax.ppermute(values, 'tensor', [(i, i ^ 2) for i in range(size)])]
    unnamed x12 -> x8, waiting for transfers between devices: 2.34 us -> 171 us
    all_gather x4 -> x0, waiting for transfers between devices: 119 us -> none  [the longest x1 35 us: body(): mixer_grad = lax.all_gather(mixer_grad_part, 'tensor', axis=1, tiled=True)]
    unnamed x72 -> x264, local copies, waits for them, and re-layouts: 8.08 us -> 51.6 us
    psum x4 -> x0, blocking collectives: 40.8 us -> none  [the longest x1 22.9 us: body(): lax.psum((grad_gain_one, grad_gain_two, grad_taps), 'dp')]
    ppermute x0 -> x57, starting transfers between devices: none -> 36.2 us  [the longest x21 19.8 us: swap_chip(): return lax.ppermute(values, 'tensor', [(i, i ^ 2) for i in range(size)])]
    while x25 -> x0, local copies, waits for them, and re-layouts: 20.7 us -> none
  transfers between devices with their start and end apart: 12 -> 61, of which waited for: 12 -> 30; matrix products, arithmetic and copies ran while one was open for 6% -> 21% of each run, Pallas kernels for 0% -> 0%
where the time goes in v1:
time: 622 us; the launch traced here: 613 us
  waiting for transfers between devices  340 us (55%)
  matrix products  113 us (18%)
  local copies, waits for them, and re-layouts  65.4 us (11%)
  other arithmetic  41.1 us (7%)
  starting transfers between devices  36.7 us (6%)
  between operations  16.1 us (3%)
    unnamed x8, waiting for transfers between devices  171 us
    ppermute x21, waiting for transfers between devices, swap_chip(): return lax.ppermute(values, 'tensor', [(i, i ^ 2) for i in range(size)])  155 us
    unnamed x264, local copies, waits for them, and re-layouts  51.6 us
    dot_general x4, matrix products, dot_last(): lax.dot_general(left, right, (((1,), (1,)), ((), ())), preferred_element_...  23.2 us
    ppermute x21, starting transfers between devices, swap_chip(): return lax.ppermute(values, 'tensor', [(i, i ^ 2) for i in range(size)])  19.8 us
    dot_general x2, matrix products, body(): jnp.einsum('td,ktf->kdf', normed_two[k], gu_grad[k], preferred_element_ty...  18.6 us
    select_n x20, other arithmetic, ordered(): jnp.where(is_first, jnp.concatenate([own, other], axis=-1), jnp.concatena...  17.4 us
    dot_general x2, matrix products, body(): jnp.einsum('td,kdf->ktf', normed_two[k], weight_feed, preferred_element_t...  16.1 us
  transfers between devices with their start and end apart: 61, of which 30 were waited for; matrix products, arithmetic and copies ran while one was open for 21% of the time, Pallas kernels for 0%

profile of v1, /device:TPU:0, one launch (start us, length us, event | category | flops | bytes accessed | tf_op | source)
XLA Modules:
  0.0 612.6 jit_solution(3048589288511503435)
XLA Ops:
  25.0 3.4 collective-permute-done.1
  28.5 10.8 %collective-permute-done.4 = bf16[1024,256]{0,1:T(8,128)(2,1)} collective-permute-done((bf16[1024,256]{0,1:T(8,128)(2,1)S(1)}, bf16[1024,256]{0,1:T(8,128)(2,1)}, u32[]{:S(2)}, u32[]{:S(2)}) %collective-permute-start.4) | collective-permute-done | bytes 524320 | tf_op jit(solution)/shard_map/ppermute | solution.py:19
  63.3 11.4 %collective-permute-done.17 = bf16[1024,256]{0,1:T(8,128)(2,1)S(1)} collective-permute-done((bf16[1024,256]{0,1:T(8,128)(2,1)S(1)}, bf16[1024,256]{0,1:T(8,128)(2,1)S(1)}, u32[]{:S(2)}, u32[]{:S(2)}) %collective-permute-start.17) | collective-permute-done | bytes 524320 | tf_op jit(solution)/shard_map/ppermute | solution.py:19
  76.8 9.1 %collective-permute-done.34 = bf16[1024,256]{0,1:T(8,128)(2,1)S(1)} collective-permute-done((bf16[1024,256]{0,1:T(8,128)(2,1)S(1)}, bf16[1024,256]{0,1:T(8,128)(2,1)S(1)}, u32[]{:S(2)}, u32[]{:S(2)}) %collective-permute-start.34) | collective-permute-done | bytes 524320 | tf_op jit(solution)/shard_map/ppermute | solution.py:19
  88.0 8.6 %collective-permute-done.19 = bf16[1024,256]{0,1:T(8,128)(2,1)S(1)} collective-permute-done((bf16[1024,256]{0,1:T(8,128)(2,1)S(1)}, bf16[1024,256]{0,1:T(8,128)(2,1)S(1)}, u32[]{:S(2)}, u32[]{:S(2)}) %collective-permute-start.19) | collective-permute-done | bytes 524320 | tf_op jit(solution)/shard_map/ppermute | solution.py:19
  102.2 8.1 %convolution_bitcast_fusion = f32[2,1024,1152]{2,1,0:T(8,128)} fusion(bf16[2,1024,1152]{2,1,0:T(8,128)(2,1)S(1)} %bitcast.247, f32[1024]{0:T(1024)S(1)} %add_rsqrt_fusion, f32[1024]{0:T(1024)S(1)} %bitcast.274, bf16[1024,512]{0,1:T(8,128)(2,1)S(1)} %maximum_select_fusion.15, bf16[1024,512]{0,1:T(8,128)(2,1)S(1)} %maximum_select_fusion.14, pred[]{:T(512)S(6)} %eq.10), kind=kOutput, calls=%fused_computation.1 | convolution fusion | flops 4845469696 | bytes 16261121 | tf_op jit(solution)/shard_map/td,kdf->ktf/dot_general | solution.py:164
  110.3 10.2 %convert_bitcast_fusion.1 = (bf16[1,1024,1152]{2,1,0:T(8,128)(2,1)}, bf16[1,1024,1152]{2,1,0:T(8,128)(2,1)}, f32[1024]{0:T(1024)S(1)}, bf16[1024,1152]{1,0:T(8,128)(2,1)}) fusion(f32[2,1024,1152]{2,1,0:T(8,128)} %convolution_bitcast_fusion, bf16[1152,1024]{1,0:T(8,128)(2,1)S(1)} %copy-done.26, bf16[1024,512]{0,1:T(8,128)(2,1)} %maximum_select_fusion.21, ...), kind=kOutput, calls=%fused_computation.45 | convolution fusion | flops 2448817152 | bytes 20976640 | tf_op jit(solution)/shard_map/dot_general | solution.py:82
  120.5 3.6 convolution_convert_fusion
  124.7 5.2 bitcast_convert_fusion.2
  132.6 5.0 bitcast_add_fusion.2
  141.0 16.4 %collective-permute-done.39 = f32[1024]{0:T(1024)S(1)} collective-permute-done((f32[1024]{0:T(1024)S(1)}, f32[1024]{0:T(1024)S(1)}, u32[]{:S(2)}, u32[]{:S(2)}) %collective-permute-start.39) | collective-permute-done | bytes 4128 | tf_op jit(solution)/shard_map/ppermute | solution.py:19
  159.9 13.2 %collective-permute-done.41 = bf16[1024,256]{0,1:T(8,128)(2,1)S(1)} collective-permute-done((bf16[1024,256]{0,1:T(8,128)(2,1)S(1)}, bf16[1024,256]{0,1:T(8,128)(2,1)S(1)}, u32[]{:S(2)}, u32[]{:S(2)}) %collective-permute-start.41) | collective-permute-done | bytes 524320 | tf_op jit(solution)/shard_map/ppermute | solution.py:19
  187.1 12.7 %collective-permute-done.10 = bf16[1024,256]{0,1:T(8,128)(2,1)S(1)} collective-permute-done((bf16[1024,256]{0,1:T(8,128)(2,1)S(1)}, bf16[1024,256]{0,1:T(8,128)(2,1)S(1)}, u32[]{:S(2)}, u32[]{:S(2)}) %collective-permute-start.10) | collective-permute-done | bytes 524320 | tf_op jit(solution)/shard_map/ppermute | solution.py:19
  200.4 10.6 %collective-permute-done.24 = bf16[1024,256]{0,1:T(8,128)(2,1)S(1)} collective-permute-done((bf16[1024,256]{0,1:T(8,128)(2,1)S(1)}, bf16[1024,256]{0,1:T(8,128)(2,1)S(1)}, u32[]{:S(2)}, u32[]{:S(2)}) %collective-permute-start.24) | collective-permute-done | bytes 524320 | tf_op jit(solution)/shard_map/ppermute | solution.py:19
  211.6 9.9 %collective-permute-done.12 = bf16[1024,256]{0,1:T(8,128)(2,1)S(1)} collective-permute-done((bf16[1024,256]{0,1:T(8,128)(2,1)S(1)}, bf16[1024,256]{0,1:T(8,128)(2,1)S(1)}, u32[]{:S(2)}, u32[]{:S(2)}) %collective-permute-start.12) | collective-permute-done | bytes 524320 | tf_op jit(solution)/shard_map/ppermute | solution.py:19
  224.9 8.1 %convolution_bitcast_fusion.1 = f32[2,1024,1152]{2,1,0:T(8,128)} fusion(bf16[2,1024,1152]{2,1,0:T(8,128)(2,1)S(1)} %bitcast.247, f32[1024]{0:T(1024)S(1)} %bitcast.275, f32[1024]{0:T(1024)S(1)} %add_rsqrt_fusion.2, bf16[1024,512]{0,1:T(8,128)(2,1)S(1)} %maximum_select_fusion.13, bf16[1024,512]{0,1:T(8,128)(2,1)S(1)} %maximum_select_fusion.12, pred[]{:T(512)S(6)} %eq.10), kind=kOutput, calls=%fused_computation.2 | convolution fusion | flops 4845469696 | bytes 16261121 | tf_op jit(solution)/shard_map/td,kdf->ktf/dot_general | solution.py:164
  233.0 9.9 %convert_bitcast_fusion.3 = (bf16[1,1024,1152]{2,1,0:T(8,128)(2,1)S(1)}, bf16[1,1024,1152]{2,1,0:T(8,128)(2,1)}, f32[1024]{0:T(1024)S(1)}, bf16[1024,1152]{1,0:T(8,128)(2,1)}) fusion(f32[2,1024,1152]{2,1,0:T(8,128)} %convolution_bitcast_fusion.1, bf16[1152,1024]{1,0:T(8,128)(2,1)S(1)} %copy-done.26, bf16[1024,512]{0,1:T(8,128)(2,1)S(1)} %maximum_select_fusion.17, ...), kind=kOutput, calls=%fused_computation.47 | convolution fusion | flops 2448817152 | bytes 20976640 | tf_op jit(solution)/shard_map/dot_general | solution.py:82
  244.3 4.5 bitcast_convert_fusion.3
  259.6 20.1 %collective-permute-done.29 = f32[1024]{0:T(1024)S(1)} collective-permute-done((f32[1024]{0:T(1024)S(1)}, f32[1024]{0:T(1024)S(1)}, u32[]{:S(2)}, u32[]{:S(2)}) %collective-permute-start.29) | collective-permute-done | bytes 4128 | tf_op jit(solution)/shard_map/ppermute | solution.py:19
  281.7 12.9 %collective-permute-done.31 = bf16[1024,256]{0,1:T(8,128)(2,1)S(1)} collective-permute-done((bf16[1024,256]{0,1:T(8,128)(2,1)S(1)}, bf16[1024,256]{0,1:T(8,128)(2,1)S(1)}, u32[]{:S(2)}, u32[]{:S(2)}) %collective-permute-start.31) | collective-permute-done | bytes 524320 | tf_op jit(solution)/shard_map/ppermute | solution.py:19
  302.1 5.8 fusion.78
  308.0 5.3 add_convert_fusion.1
  313.3 4.4 copy.169
  339.3 8.4 %fusion.22 = f32[2,1152,1024]{2,1,0:T(8,128)S(1)} fusion(bf16[1,1024,1152]{2,1,0:T(8,128)(2,1)} %get-tuple-element.69, bf16[1,1024,1152]{2,1,0:T(8,128)(2,1)} %copy-done.118, f32[1024]{0:T(1024)S(1)} %bitcast.276, f32[1024]{0:T(1024)S(1)} %add_rsqrt_fusion.2, bf16[1024,512]{0,1:T(8,128)(2,1)} %copy-done.23, bf16[1024,512]{0,1:T(8,128)(2,1)S(1)} %copy-done.22, ...), kind=kOutput, calls=%fused_computation.84 | convolution fusion | flops 4847828992 | bytes 16261121 | tf_op jit(solution)/shard_map/td,ktf->kdf/dot_general | solution.py:188
  347.8 10.1 %fusion.2 = bf16[2,1024,1152]{1,2,0:T(8,128)(2,1)} fusion(f32[2,1152,1024]{2,1,0:T(8,128)S(1)} %fusion.22, bf16[1,1024,1152]{2,1,0:T(8,128)(2,1)} %get-tuple-element.72, bf16[1,1024,1152]{2,1,0:T(8,128)(2,1)} %get-tuple-element.71, f32[1024]{0:T(1024)S(1)} %copy-done.89, f32[1024]{0:T(1024)S(1)} %bitcast.277, bf16[1024,512]{0,1:T(8,128)(2,1)S(1)} %copy-done.20, ...), kind=kOutput, calls=%fused_computation.28 | convolution fusion | flops 4852547584 | bytes 20979712 | tf_op jit(solution)/shard_map/td,ktf->kdf/dot_general | solution.py:188
  357.9 12.9 %copy.167 = bf16[2,1024,1152]{2,0,1:T(2,128)(2,1)} copy(bf16[2,1024,1152]{1,2,0:T(8,128)(2,1)} %fusion.2) | data formatting | bytes 9437184
  370.8 5.4 copy.176
  391.4 9.2 %collective-permute-done.48 = bf16[1024,256]{0,1:T(8,128)(2,1)S(1)} collective-permute-done((bf16[1024,256]{0,1:T(8,128)(2,1)S(1)}, bf16[1024,256]{0,1:T(8,128)(2,1)S(1)}, u32[]{:S(2)}, u32[]{:S(2)}) %collective-permute-start.48) | collective-permute-done | bytes 524320 | tf_op jit(solution)/shard_map/ppermute | solution.py:19
  405.3 5.7 collective-permute-done.46
  427.0 9.2 %reduce-scatter.19.cloned.1.call-done = bf16[128,1152]{1,0:T(8,128)(2,1)} async-done(((bf16[1024,1152]{1,0:T(8,128)(2,1)}), bf16[128,1152]{1,0:T(8,128)(2,1)}) %reduce-scatter.19.cloned.1.call-update) | async-done | bytes 294928
  438.2 65.7 %reduce-scatter.13.cloned.1.call-done = bf16[128,768]{1,0:T(8,128)(2,1)} async-done(((bf16[1024,768]{1,0:T(8,128)(2,1)}), bf16[128,768]{1,0:T(8,128)(2,1)}) %reduce-scatter.13.cloned.1.call-update) | async-done | bytes 196624
  506.1 95.7 %reduce-scatter.17.cloned.1.call-done = bf16[128,2304]{1,0:T(8,128)(2,1)} async-done(((bf16[1024,2304]{1,0:T(8,128)(2,1)}), bf16[128,2304]{1,0:T(8,128)(2,1)}) %reduce-scatter.17.cloned.1.call-update) | async-done | bytes 589840
  (505 shorter events, 164.5 us)
Async XLA Ops:
  7.2 413.1 %reduce-scatter.15.cloned.1.call-start = ((), (), s32[]{:S(2)}) async-start(), calls=%async_computation.5 | async-start | bytes 589824
  9.1 13.1 %collective-permute-start.7 = (bf16[2,256]{1,0:T(2,128)(2,1)}, bf16[2,256]{1,0:T(2,128)(2,1)}, u32[]{:S(2)}, u32[]{:S(2)}) collective-permute-start(bf16[2,256]{1,0:T(2,128)(2,1)} %pad_maximum_fusion.47), channel_id=1, source_target_pairs={{0,2},{1,3},{2,0},{3,1},{4,6},{5,7},{6,4},{7,5},{8,10},{9,11},{10,... | collective-permute-start | bytes 3080 | tf_op jit(solution)/shard_map/ppermute | solution.py:19
  13.6 14.9 %collective-permute-start.1 = (bf16[1024,256]{0,1:T(8,128)(2,1)S(1)}, bf16[1024,256]{0,1:T(8,128)(2,1)}, u32[]{:S(2)}, u32[]{:S(2)}) collective-permute-start(bf16[1024,256]{0,1:T(8,128)(2,1)S(1)} %copy.171), channel_id=1, source_target_pairs={{0,2},{1,3},{2,0},{3,1},{4,6},{5,7},{6,4},{7,5},{8,10},{9,11},{10,... | collective-permute-start | bytes 1572872 | tf_op jit(solution)/shard_map/ppermute | solution.py:19
  13.8 25.6 %collective-permute-start = (bf16[1024,256]{0,1:T(8,128)(2,1)S(1)}, bf16[1024,256]{0,1:T(8,128)(2,1)}, u32[]{:S(2)}, u32[]{:S(2)}) collective-permute-start(bf16[1024,256]{0,1:T(8,128)(2,1)S(1)} %copy.171), channel_id=1, source_target_pairs={{0,1},{1,0},{2,3},{3,2},{4,5},{5,4},{6,7},{7,6},{8,9},{9,8},{10,11... | collective-permute-start | bytes 1572872 | tf_op jit(solution)/shard_map/ppermute | solution.py:14
  14.5 24.9 %collective-permute-start.4 = (bf16[1024,256]{0,1:T(8,128)(2,1)S(1)}, bf16[1024,256]{0,1:T(8,128)(2,1)}, u32[]{:S(2)}, u32[]{:S(2)}) collective-permute-start(bf16[1024,256]{0,1:T(8,128)(2,1)S(1)} %copy.174), channel_id=1, source_target_pairs={{0,2},{1,3},{2,0},{3,1},{4,6},{5,7},{6,4},{7,5},{8,10},{9,11},{10,... | collective-permute-start | bytes 1572872 | tf_op jit(solution)/shard_map/ppermute | solution.py:19
  22.2 18.8 %collective-permute-start.3 = (bf16[1024,256]{0,1:T(8,128)(2,1)S(1)}, bf16[1024,256]{0,1:T(8,128)(2,1)S(1)}, u32[]{:S(2)}, u32[]{:S(2)}) collective-permute-start(bf16[1024,256]{0,1:T(8,128)(2,1)S(1)} %copy.174), channel_id=1, source_target_pairs={{0,1},{1,0},{2,3},{3,2},{4,5},{5,4},{6,7},{7,6},{8,9},{9,8},{10,11... | collective-permute-start | bytes 1572872 | tf_op jit(solution)/shard_map/ppermute | solution.py:14
  28.5 13.0 %collective-permute-start.2 = (bf16[1024,256]{0,1:T(8,128)(2,1)}, bf16[1024,256]{0,1:T(8,128)(2,1)S(1)}, u32[]{:S(2)}, u32[]{:S(2)}) collective-permute-start(bf16[1024,256]{0,1:T(8,128)(2,1)} %collective-permute-done.1), channel_id=1, source_target_pairs={{0,1},{1,0},{2,3},{3,2},{4,5},{5,4},{6,7},{7,6},{8,9},{9,8},{10,11... | collective-permute-start | bytes 1572872 | tf_op jit(solution)/shard_map/ppermute | solution.py:14
  59.9 14.8 %collective-permute-start.17 = (bf16[1024,256]{0,1:T(8,128)(2,1)S(1)}, bf16[1024,256]{0,1:T(8,128)(2,1)S(1)}, u32[]{:S(2)}, u32[]{:S(2)}) collective-permute-start(bf16[1024,256]{0,1:T(8,128)(2,1)S(1)} %slice.566), channel_id=1, source_target_pairs={{0,2},{1,3},{2,0},{3,1},{4,6},{5,7},{6,4},{7,5},{8,10},{9,11},{10,... | collective-permute-start | bytes 1572872 | tf_op jit(solution)/shard_map/ppermute | solution.py:19
  61.5 24.4 %collective-permute-start.34 = (bf16[1024,256]{0,1:T(8,128)(2,1)S(1)}, bf16[1024,256]{0,1:T(8,128)(2,1)S(1)}, u32[]{:S(2)}, u32[]{:S(2)}) collective-permute-start(bf16[1024,256]{0,1:T(8,128)(2,1)S(1)} %copy-done.13), channel_id=1, source_target_pairs={{0,2},{1,3},{2,0},{3,1},{4,6},{5,7},{6,4},{7,5},{8,10},{9,11},{10,... | collective-permute-start | bytes 1572872 | tf_op jit(solution)/shard_map/ppermute | solution.py:19
  75.0 21.6 %collective-permute-start.19 = (bf16[1024,256]{0,1:T(8,128)(2,1)S(1)}, bf16[1024,256]{0,1:T(8,128)(2,1)S(1)}, u32[]{:S(2)}, u32[]{:S(2)}) collective-permute-start(bf16[1024,256]{0,1:T(8,128)(2,1)S(1)} %get-tuple-element.64), channel_id=1, source_target_pairs={{0,2},{1,3},{2,0},{3,1},{4,6},{5,7},{6,4},{7,5},{8,10},{9,11},{10,... | collective-permute-start | bytes 1572872 | tf_op jit(solution)/shard_map/ppermute | solution.py:19
  76.8 20.4 %collective-permute-start.33 = (bf16[1024,256]{0,1:T(8,128)(2,1)S(1)}, bf16[1024,256]{0,1:T(8,128)(2,1)S(1)}, u32[]{:S(2)}, u32[]{:S(2)}) collective-permute-start(bf16[1024,256]{0,1:T(8,128)(2,1)S(1)} %copy-done.13), channel_id=1, source_target_pairs={{0,1},{1,0},{2,3},{3,2},{4,5},{5,4},{6,7},{7,6},{8,9},{9,8},{10,11... | collective-permute-start | bytes 1572872 | tf_op jit(solution)/shard_map/ppermute | solution.py:14
  85.9 14.2 %collective-permute-start.18 = (bf16[1024,256]{0,1:T(8,128)(2,1)S(1)}, bf16[1024,256]{0,1:T(8,128)(2,1)S(1)}, u32[]{:S(2)}, u32[]{:S(2)}) collective-permute-start(bf16[1024,256]{0,1:T(8,128)(2,1)S(1)} %get-tuple-element.64), channel_id=1, source_target_pairs={{0,1},{1,0},{2,3},{3,2},{4,5},{5,4},{6,7},{7,6},{8,9},{9,8},{10,11... | collective-permute-start | bytes 1572872 | tf_op jit(solution)/shard_map/ppermute | solution.py:14
  131.7 25.7 %collective-permute-start.22 = (bf16[1024,256]{0,1:T(8,128)(2,1)S(1)}, bf16[1024,256]{0,1:T(8,128)(2,1)S(1)}, u32[]{:S(2)}, u32[]{:S(2)}) collective-permute-start(bf16[1024,256]{0,1:T(8,128)(2,1)S(1)} %slice.565), channel_id=1, source_target_pairs={{0,2},{1,3},{2,0},{3,1},{4,6},{5,7},{6,4},{7,5},{8,10},{9,11},{10,... | collective-permute-start | bytes 1572872 | tf_op jit(solution)/shard_map/ppermute | solution.py:19
  137.7 19.6 %collective-permute-start.37 = (bf16[1024,256]{0,1:T(8,128)(2,1)S(1)}, bf16[1024,256]{0,1:T(8,128)(2,1)S(1)}, u32[]{:S(2)}, u32[]{:S(2)}) collective-permute-start(bf16[1024,256]{0,1:T(8,128)(2,1)S(1)} %slice.563), channel_id=1, source_target_pairs={{0,2},{1,3},{2,0},{3,1},{4,6},{5,7},{6,4},{7,5},{8,10},{9,11},{10,... | collective-permute-start | bytes 1572872 | tf_op jit(solution)/shard_map/ppermute | solution.py:19
  140.1 17.2 %collective-permute-start.39 = (f32[1024]{0:T(1024)S(1)}, f32[1024]{0:T(1024)S(1)}, u32[]{:S(2)}, u32[]{:S(2)}) collective-permute-start(f32[1024]{0:T(1024)S(1)} %add.380), channel_id=1, source_target_pairs={{0,2},{1,3},{2,0},{3,1},{4,6},{5,7},{6,4},{7,5},{8,10},{9,11},{10,... | collective-permute-start | bytes 12296 | tf_op jit(solution)/shard_map/ppermute | solution.py:19
  159.6 13.5 %collective-permute-start.41 = (bf16[1024,256]{0,1:T(8,128)(2,1)S(1)}, bf16[1024,256]{0,1:T(8,128)(2,1)S(1)}, u32[]{:S(2)}, u32[]{:S(2)}) collective-permute-start(bf16[1024,256]{0,1:T(8,128)(2,1)S(1)} %get-tuple-element.58), channel_id=1, source_target_pairs={{0,2},{1,3},{2,0},{3,1},{4,6},{5,7},{6,4},{7,5},{8,10},{9,11},{10,... | collective-permute-start | bytes 1572872 | tf_op jit(solution)/shard_map/ppermute | solution.py:19
  159.9 13.3 %collective-permute-start.40 = (bf16[1024,256]{0,1:T(8,128)(2,1)S(1)}, bf16[1024,256]{0,1:T(8,128)(2,1)S(1)}, u32[]{:S(2)}, u32[]{:S(2)}) collective-permute-start(bf16[1024,256]{0,1:T(8,128)(2,1)S(1)} %get-tuple-element.58), channel_id=1, source_target_pairs={{0,1},{1,0},{2,3},{3,2},{4,5},{5,4},{6,7},{7,6},{8,9},{9,8},{10,11... | collective-permute-start | bytes 1572872 | tf_op jit(solution)/shard_map/ppermute | solution.py:14
  185.0 14.8 %collective-permute-start.10 = (bf16[1024,256]{0,1:T(8,128)(2,1)S(1)}, bf16[1024,256]{0,1:T(8,128)(2,1)S(1)}, u32[]{:S(2)}, u32[]{:S(2)}) collective-permute-start(bf16[1024,256]{0,1:T(8,128)(2,1)S(1)} %slice.568), channel_id=1, source_target_pairs={{0,2},{1,3},{2,0},{3,1},{4,6},{5,7},{6,4},{7,5},{8,10},{9,11},{10,... | collective-permute-start | bytes 1572872 | tf_op jit(solution)/shard_map/ppermute | solution.py:19
  185.3 25.7 %collective-permute-start.24 = (bf16[1024,256]{0,1:T(8,128)(2,1)S(1)}, bf16[1024,256]{0,1:T(8,128)(2,1)S(1)}, u32[]{:S(2)}, u32[]{:S(2)}) collective-permute-start(bf16[1024,256]{0,1:T(8,128)(2,1)S(1)} %copy-done.12), channel_id=1, source_target_pairs={{0,2},{1,3},{2,0},{3,1},{4,6},{5,7},{6,4},{7,5},{8,10},{9,11},{10,... | collective-permute-start | bytes 1572872 | tf_op jit(solution)/shard_map/ppermute | solution.py:19
  200.1 21.4 %collective-permute-start.12 = (bf16[1024,256]{0,1:T(8,128)(2,1)S(1)}, bf16[1024,256]{0,1:T(8,128)(2,1)S(1)}, u32[]{:S(2)}, u32[]{:S(2)}) collective-permute-start(bf16[1024,256]{0,1:T(8,128)(2,1)S(1)} %get-tuple-element.60), channel_id=1, source_target_pairs={{0,2},{1,3},{2,0},{3,1},{4,6},{5,7},{6,4},{7,5},{8,10},{9,11},{10,... | collective-permute-start | bytes 1572872 | tf_op jit(solution)/shard_map/ppermute | solution.py:19
  200.4 21.1 %collective-permute-start.23 = (bf16[1024,256]{0,1:T(8,128)(2,1)S(1)}, bf16[1024,256]{0,1:T(8,128)(2,1)S(1)}, u32[]{:S(2)}, u32[]{:S(2)}) collective-permute-start(bf16[1024,256]{0,1:T(8,128)(2,1)S(1)} %copy-done.12), channel_id=1, source_target_pairs={{0,1},{1,0},{2,3},{3,2},{4,5},{5,4},{6,7},{7,6},{8,9},{9,8},{10,11... | collective-permute-start | bytes 1572872 | tf_op jit(solution)/shard_map/ppermute | solution.py:14
  254.2 25.5 %collective-permute-start.27 = (bf16[1024,256]{0,1:T(8,128)(2,1)S(1)}, bf16[1024,256]{0,1:T(8,128)(2,1)S(1)}, u32[]{:S(2)}, u32[]{:S(2)}) collective-permute-start(bf16[1024,256]{0,1:T(8,128)(2,1)S(1)} %slice.564), channel_id=1, source_target_pairs={{0,2},{1,3},{2,0},{3,1},{4,6},{5,7},{6,4},{7,5},{8,10},{9,11},{10,... | collective-permute-start | bytes 1572872 | tf_op jit(solution)/shard_map/ppermute | solution.py:19
  256.3 23.4 %collective-permute-start.15 = (bf16[1024,256]{0,1:T(8,128)(2,1)S(1)}, bf16[1024,256]{0,1:T(8,128)(2,1)S(1)}, u32[]{:S(2)}, u32[]{:S(2)}) collective-permute-start(bf16[1024,256]{0,1:T(8,128)(2,1)S(1)} %slice.567), channel_id=1, source_target_pairs={{0,2},{1,3},{2,0},{3,1},{4,6},{5,7},{6,4},{7,5},{8,10},{9,11},{10,... | collective-permute-start | bytes 1572872 | tf_op jit(solution)/shard_map/ppermute | solution.py:19
  259.3 20.4 %collective-permute-start.29 = (f32[1024]{0:T(1024)S(1)}, f32[1024]{0:T(1024)S(1)}, u32[]{:S(2)}, u32[]{:S(2)}) collective-permute-start(f32[1024]{0:T(1024)S(1)} %add.373), channel_id=1, source_target_pairs={{0,2},{1,3},{2,0},{3,1},{4,6},{5,7},{6,4},{7,5},{8,10},{9,11},{10,... | collective-permute-start | bytes 12296 | tf_op jit(solution)/shard_map/ppermute | solution.py:19
  281.4 13.2 %collective-permute-start.31 = (bf16[1024,256]{0,1:T(8,128)(2,1)S(1)}, bf16[1024,256]{0,1:T(8,128)(2,1)S(1)}, u32[]{:S(2)}, u32[]{:S(2)}) collective-permute-start(bf16[1024,256]{0,1:T(8,128)(2,1)S(1)} %get-tuple-element.54), channel_id=1, source_target_pairs={{0,2},{1,3},{2,0},{3,1},{4,6},{5,7},{6,4},{7,5},{8,10},{9,11},{10,... | collective-permute-start | bytes 1572872 | tf_op jit(solution)/shard_map/ppermute | solution.py:19
  281.7 13.8 %collective-permute-start.30 = (bf16[1024,256]{0,1:T(8,128)(2,1)S(1)}, bf16[1024,256]{0,1:T(8,128)(2,1)S(1)}, u32[]{:S(2)}, u32[]{:S(2)}) collective-permute-start(bf16[1024,256]{0,1:T(8,128)(2,1)S(1)} %get-tuple-element.54), channel_id=1, source_target_pairs={{0,1},{1,0},{2,3},{3,2},{4,5},{5,4},{6,7},{7,6},{8,9},{9,8},{10,11... | collective-permute-start | bytes 1572872 | tf_op jit(solution)/shard_map/ppermute | solution.py:14
  301.8 134.4 %reduce-scatter.19.cloned.1.call-start = ((), (), s32[]{:S(2)}) async-start(), calls=%async_computation.7 | async-start | bytes 2654208
  317.7 186.2 %reduce-scatter.13.cloned.1.call-start = ((), (), s32[]{:S(2)}) async-start(), calls=%async_computation.4 | async-start | bytes 1769472
  339.0 262.8 %reduce-scatter.17.cloned.1.call-start = ((), (), s32[]{:S(2)}) async-start(), calls=%async_computation.6 | async-start | bytes 5308416
  385.7 14.8 %collective-permute-start.48 = (bf16[1024,256]{0,1:T(8,128)(2,1)S(1)}, bf16[1024,256]{0,1:T(8,128)(2,1)S(1)}, u32[]{:S(2)}, u32[]{:S(2)}) collective-permute-start(bf16[1024,256]{0,1:T(8,128)(2,1)S(1)} %slice.561), channel_id=1, source_target_pairs={{0,2},{1,3},{2,0},{3,1},{4,6},{5,7},{6,4},{7,5},{8,10},{9,11},{10,... | collective-permute-start | bytes 1572872 | tf_op jit(solution)/shard_map/ppermute | solution.py:19
  388.0 15.6 %collective-permute-start.54 = (f32[4,256]{1,0:T(4,128)S(1)}, f32[4,256]{1,0:T(4,128)S(1)}, u32[]{:S(2)}, u32[]{:S(2)}) collective-permute-start(f32[4,256]{1,0:T(4,128)S(1)} %pad_maximum_fusion.46), channel_id=1, source_target_pairs={{0,4},{4,0},{8,12},{12,8},{16,20},{20,16},{24,28},{28,24},{1,5},{5... | collective-permute-start | bytes 12296 | tf_op jit(solution)/shard_map/ppermute | solution.py:65
  390.7 20.3 %collective-permute-start.44 = (bf16[1024,256]{0,1:T(8,128)(2,1)S(1)}, bf16[1024,256]{0,1:T(8,128)(2,1)S(1)}, u32[]{:S(2)}, u32[]{:S(2)}) collective-permute-start(bf16[1024,256]{0,1:T(8,128)(2,1)S(1)} %slice.562), channel_id=1, source_target_pairs={{0,2},{1,3},{2,0},{3,1},{4,6},{5,7},{6,4},{7,5},{8,10},{9,11},{10,... | collective-permute-start | bytes 1572872 | tf_op jit(solution)/shard_map/ppermute | solution.py:19
  (154 other events, 1516.8 us)
Sparse Core Ops, SparseCore 0:
  301.9 62.3 reduce-scatter.14
  368.2 67.9 reduce-scatter.18
  440.0 63.8 reduce-scatter.12
  507.4 94.3 reduce-scatter.16

commit v2 on v1

--- a/solution.py
+++ b/solution.py
@@ -47,10 +47,20 @@
     return sent, kept
 
 
-def scatter_columns(sent, kept):
-    total = kept + swap_core(sent.astype(BF16)).astype(F32)
-    width = total.shape[1] // 2
-    return total[:, width:] + swap_chip(total[:, :width].astype(BF16)).astype(F32)
+def after(values, *others):
+    return lax.optimization_barrier((values,) + others)[0]
+
+
+def scatter_all(pairs, *others):
+    kept_last = tuple(kept for sent, kept in pairs)
+    results = []
+    for k, (sent, kept) in enumerate(pairs):
+        total = kept + swap_core(sent).astype(F32)
+        width = total.shape[1] // 2
+        received = swap_chip(total[:, :width].astype(BF16))
+        received = after(received, *kept_last[k + 1 :], *others)
+        results.append(total[:, width:] + received.astype(F32))
+    return results
 
 
 def sum_tensor(values):
@@ -65,6 +75,22 @@
         values = values + lax.ppermute(values, "dp", [(i, i ^ step) for i in range(size)])
         step *= 2
     return values
+
+
+def scatter_groups(values):
+    size = lax.axis_size("dp")
+    index = lax.axis_index("dp")
+    block = values.shape[0] // size
+    step = 1
+    while step < size:
+        pairs = values.reshape(-1, 2, block, values.shape[-1])
+        bit = (index // step) % 2
+        sent = lax.dynamic_index_in_dim(pairs, 1 - bit, 1, keepdims=False).astype(BF16)
+        kept = lax.dynamic_index_in_dim(pairs, bit, 1, keepdims=False)
+        moved = lax.ppermute(sent, "dp", [(i, i ^ step) for i in range(size)])
+        values = kept + moved.astype(F32)
+        step *= 2
+    return values.reshape(block, -1)
 
 
 def total_of(parts):
@@ -131,7 +157,7 @@
     taps = conv_taps.astype(F32)
 
     normed_one, gates, mixed, prev_one, prev_two, conv = [], [], [], [], [], []
-    mixer_rows, middle, middle_full, scale_one = [], [], [], []
+    mixer_rows, mixer_parts, middle, middle_full, scale_one = [], [], [], [], []
     for k in span:
         wide = token_full[k].astype(F32)
         scale = lax.rsqrt(jnp.mean(wide * wide, axis=1, keepdims=True) + EPSILON)
@@ -147,16 +173,20 @@
         prev_two.append(extended[:-2] * same_two[k])
         conv.append(taps[2] * mix + taps[1] * prev_one[k] + taps[0] * prev_two[k])
         mixer_rows.append((gate[1] * conv[k]).astype(BF16))
-        mixer_out = scatter_columns(
-            jnp.dot(mixer_rows[k], out_sent, preferred_element_type=F32),
-            jnp.dot(mixer_rows[k], out_kept, preferred_element_type=F32),
-        )
+        mixer_parts.append(
+            (
+                jnp.dot(mixer_rows[k], out_sent, preferred_element_type=F32).astype(BF16),
+                jnp.dot(mixer_rows[k], out_kept, preferred_element_type=F32),
+            )
+        )
+    for k, mixer_out in enumerate(scatter_all(mixer_parts)):
         middle.append(token_parts[k].astype(F32) + live[k] * mixer_out)
         middle_full.append(gather_columns(middle[k].astype(BF16), core, chip))
 
     grad_full = [gather_columns(part, core, chip) for part in grad_later]
     normed_two, hidden, feed_grad, gu_grad, block_out = [], [], [], [], []
     middle_grad, mixer_grad, gain_two_parts = [], [], []
+    scale_two, inner_two, feed_parts = [], [], []
     for k in span:
         wide = middle_full[k].astype(F32)
         scale = lax.rsqrt(jnp.mean(wide * wide, axis=1, keepdims=True) + EPSILON)
@@ -169,12 +199,20 @@
         hidden_grad = dot_last(feed_grad[k], weight_down)
         gate_grad = hidden_grad * up * sigmoid * (1.0 + gate * (1.0 - sigmoid))
         up_grad = hidden_grad * (gate * sigmoid)
-        inner = sum_tensor(jnp.sum(gate_grad * gate + up_grad * up, axis=1))
+        scale_two.append(scale)
+        inner_two.append(sum_tensor(jnp.sum(gate_grad * gate + up_grad * up, axis=1)))
         gu_grad.append(jnp.stack([gate_grad, up_grad]).astype(BF16))
-        normed_grad = scatter_columns(
-            jnp.einsum("ktf,kdf->td", gu_grad[k], feed_sent, preferred_element_type=F32),
-            jnp.einsum("ktf,kdf->td", gu_grad[k], feed_kept, preferred_element_type=F32),
-        )
+        feed_parts.append(
+            (
+                jnp.einsum(
+                    "ktf,kdf->td", gu_grad[k], feed_sent, preferred_element_type=F32
+                ).astype(BF16),
+                jnp.einsum("ktf,kdf->td", gu_grad[k], feed_kept, preferred_element_type=F32),
+            )
+        )
+    grad_down = total_of([dot_rows(feed_grad[k], hidden[k]) for k in span])
+    for k, normed_grad in enumerate(scatter_all(feed_parts)):
+        scale, inner = scale_two[k], inner_two[k]
         unit = middle[k] * scale
         gain_two_parts.append(jnp.sum(normed_grad * unit, axis=0))
         middle_grad.append(
@@ -183,24 +221,29 @@
             * (normed_grad * gain_two.astype(F32) - unit * (inner / full_width)[:, None])
         )
         mixer_grad.append(gather_columns((middle_grad[k] * live[k]).astype(BF16), core, chip))
-    grad_feed = total_of(
-        [
-            jnp.einsum("td,ktf->kdf", normed_two[k], gu_grad[k], preferred_element_type=F32)
-            for k in span
-        ]
-    ).astype(BF16)
-    feed_shard = lax.psum_scatter(grad_feed, "dp", scatter_dimension=1, tiled=True)
-    grad_down = total_of([dot_rows(hidden[k], feed_grad[k]) for k in span]).astype(BF16)
-    down_shard = lax.psum_scatter(grad_down, "dp", scatter_dimension=1, tiled=True)
+    grad_feed = [
+        total_of([dot_rows(normed_two[k], gu_grad[k][side]) for k in span]) for side in range(2)
+    ]
+    down_parts = [
+        (
+            jnp.dot(hidden[k], down_sent, preferred_element_type=F32).astype(BF16),
+            jnp.dot(hidden[k], down_kept, preferred_element_type=F32),
+        )
+        for k in span
+    ]
+    down_shard = scatter_groups(grad_down)
+    feed_shard = [scatter_groups(part) for part in grad_feed]
+    mixer_grad = [after(mixer_grad[0], grad_down)] + [
+        after(part, *grad_feed, *[kept for sent, kept in down_parts]) for part in mixer_grad[1:]
+    ]
 
     c_grad, conv_grad = [], []
     for k in span:
         rows_grad = dot_last(mixer_grad[k], weight_out)
         c_grad.append(rows_grad * conv[k])
         conv_grad.append(rows_grad * gates[k][1])
-    grad_out_weight = total_of([dot_rows(mixer_rows[k], mixer_grad[k]) for k in span])
-    out_shard = lax.psum_scatter(
-        grad_out_weight.astype(BF16), "dp", scatter_dimension=1, tiled=True
+    out_shard = scatter_groups(
+        total_of([dot_rows(mixer_grad[k], mixer_rows[k]) for k in span])
     )
     grad_taps = jnp.stack(
         [
@@ -210,6 +253,7 @@
         ]
     )
     gates_grad, gain_one_parts, tokens_grad = [], [], []
+    inner_one, in_parts = [], []
     for k in span:
         edge = jnp.zeros((2, part_width), F32)
         last = k == CHUNKS - 1
@@ -219,34 +263,36 @@
         next_two = jnp.concatenate([(conv_grad[k] * same_two[k])[2:], after_two], axis=0)
         mixed_grad = taps[2] * conv_grad[k] + taps[1] * next_one + taps[0] * next_two
         b_grad, x_grad = mixed_grad * gates[k][2], mixed_grad * gates[k][0]
-        inner = sum_tensor(
-            jnp.sum(b_grad * gates[k][0] + c_grad[k] * gates[k][1] + x_grad * gates[k][2], axis=1)
+        inner_one.append(
+            sum_tensor(
+                jnp.sum(
+                    b_grad * gates[k][0] + c_grad[k] * gates[k][1] + x_grad * gates[k][2], axis=1
+                )
+            )
         )
         gates_grad.append(jnp.stack([b_grad, c_grad[k], x_grad]).astype(BF16))
-        normed_grad = scatter_columns(
-            jnp.einsum("gte,gde->td", gates_grad[k], in_sent, preferred_element_type=F32),
-            jnp.einsum("gte,gde->td", gates_grad[k], in_kept, preferred_element_type=F32),
-        )
+        in_parts.append(
+            (
+                jnp.einsum(
+                    "gte,gde->td", gates_grad[k], in_sent, preferred_element_type=F32
+                ).astype(BF16),
+                jnp.einsum("gte,gde->td", gates_grad[k], in_kept, preferred_element_type=F32),
+            )
+        )
+    grad_in = [
+        total_of([dot_rows(normed_one[k], gates_grad[k][side]) for k in span]) for side in range(3)
+    ]
+    in_shard = scatter_groups(jnp.concatenate(grad_in, axis=1))
+    for k, normed_grad in enumerate(scatter_all(in_parts, *grad_in)):
         unit = token_parts[k].astype(F32) * scale_one[k]
         gain_one_parts.append(jnp.sum(normed_grad * unit, axis=0))
         tokens_grad.append(
             middle_grad[k]
             + scale_one[k]
-            * (normed_grad * gain_one.astype(F32) - unit * (inner / full_width)[:, None])
-        )
-    grad_in_weight = total_of(
-        [
-            jnp.einsum("td,gte->gde", normed_one[k], gates_grad[k], preferred_element_type=F32)
-            for k in span
-        ]
-    ).astype(BF16)
-    in_shard = lax.psum_scatter(grad_in_weight, "dp", scatter_dimension=1, tiled=True)
-
-    for k in span:
-        feed_out = scatter_columns(
-            jnp.dot(hidden[k], down_sent, preferred_element_type=F32),
-            jnp.dot(hidden[k], down_kept, preferred_element_type=F32),
-        )
+            * (normed_grad * gain_one.astype(F32) - unit * (inner_one[k] / full_width)[:, None])
+        )
+
+    for k, feed_out in enumerate(scatter_all(down_parts)):
         block_out.append((middle[k] + live[k] * feed_out).astype(BF16))
 
     small = sum_groups(jnp.concatenate([total_of(gain_two_parts)[None], grad_taps], axis=0))
@@ -255,12 +301,12 @@
         jnp.concatenate(block_out, axis=0),
         jnp.concatenate([part.astype(BF16) for part in tokens_grad], axis=0),
         gain_one_sum,
-        in_shard.astype(F32),
+        jnp.stack(jnp.split(in_shard, 3, axis=1)),
         small[1:],
-        out_shard.astype(F32),
+        out_shard.T,
         small[0],
-        feed_shard.astype(F32),
-        down_shard.astype(F32),
+        jnp.stack(feed_shard),
+        down_shard.T,
     )
 
 

time: 622 us -> 506 us (0.81)
  waiting for transfers between devices: 340 us -> 196 us
  other arithmetic: 41.1 us -> 61.1 us
  starting transfers between devices: 36.7 us -> 50.8 us
  between operations: 16.1 us -> 3.48 us
  local copies, waits for them, and re-layouts: 65.4 us -> 71.9 us
    unnamed x8 -> x0, waiting for transfers between devices: 171 us -> none
    ppermute x0 -> x15, waiting for transfers between devices: none -> 105 us  [scatter_groups(): moved = lax.ppermute(sent, 'dp', [(i, i ^ step) for i in range(size)])]
    ppermute x21, waiting for transfers between devices: 155 us -> 83 us  [swap_chip(): return lax.ppermute(values, 'tensor', [(i, i ^ 2) for i in range(size)])]
    unnamed x264 -> x301, local copies, waits for them, and re-layouts: 51.6 us -> 22.4 us
    dot_general x8 -> x4, matrix products: 30.5 us -> 7.07 us  [the longest x2 5.14 us: body(): jnp.dot(hidden[k], down_sent, preferred_element_type=F32).astype(BF16)]
    ppermute x0 -> x15, starting transfers between devices: none -> 20.5 us  [scatter_groups(): moved = lax.ppermute(sent, 'dp', [(i, i ^ step) for i in range(size)])]
    dot_general x4 -> x14, matrix products: 13.7 us -> 30 us  [dot_rows(): lax.dot_general(left, right, (((0,), (0,)), ((), ())), preferred_element_...]
    ppermute x30, waiting for transfers between devices: 13.5 us -> 0.54 us  [swap_core(): return lax.ppermute(values, 'tensor', [(i, i ^ 1) for i in range(size)])]
  transfers between devices with their start and end apart: 61 -> 72, of which waited for: 30 -> 28; matrix products, arithmetic and copies ran while one was open for 21% -> 35% of each run, Pallas kernels for 0% -> 0%
where the time goes in v2:
time: 506 us; the launch traced here: 496 us
  waiting for transfers between devices  196 us (39%)
  matrix products  113 us (22%)
  local copies, waits for them, and re-layouts  71.9 us (14%)
  other arithmetic  61.1 us (12%)
  starting transfers between devices  50.8 us (10%)
    ppermute x15, waiting for transfers between devices, scatter_groups(): moved = lax.ppermute(sent, 'dp', [(i, i ^ step) for i in range(size)])  105 us
    ppermute x21, waiting for transfers between devices, swap_chip(): return lax.ppermute(values, 'tensor', [(i, i ^ 2) for i in range(size)])  83 us
    dot_general x14, matrix products, dot_rows(): lax.dot_general(left, right, (((0,), (0,)), ((), ())), preferred_element_...  30 us
    unnamed x301, local copies, waits for them, and re-layouts  22.4 us
    dot_general x4, matrix products, dot_last(): lax.dot_general(left, right, (((1,), (1,)), ((), ())), preferred_element_...  22.3 us
    ppermute x15, starting transfers between devices, scatter_groups(): moved = lax.ppermute(sent, 'dp', [(i, i ^ step) for i in range(size)])  20.5 us
    ppermute x21, starting transfers between devices, swap_chip(): return lax.ppermute(values, 'tensor', [(i, i ^ 2) for i in range(size)])  20.5 us
    select_n x22, other arithmetic, ordered(): jnp.where(is_first, jnp.concatenate([own, other], axis=-1), jnp.concatena...  18.8 us
  transfers between devices with their start and end apart: 72, of which 28 were waited for; matrix products, arithmetic and copies ran while one was open for 35% of the time, Pallas kernels for 0%

profile of v2, /device:TPU:0, one launch (start us, length us, event | category | flops | bytes accessed | tf_op | source)
XLA Modules:
  0.0 496.1 jit_solution(1915510394276394613)
XLA Ops:
  14.4 3.7 collective-permute-done.7
  21.6 6.9 %collective-permute-done.1 = bf16[1024,256]{0,1:T(8,128)(2,1)} collective-permute-done((bf16[1024,256]{0,1:T(8,128)(2,1)S(1)}, bf16[1024,256]{0,1:T(8,128)(2,1)}, u32[]{:S(2)}, u32[]{:S(2)}) %collective-permute-start.1) | collective-permute-done | bytes 524320 | tf_op jit(solution)/shard_map/ppermute | solution.py:19
  70.4 8.1 %collective-permute-done.24 = bf16[1024,256]{0,1:T(8,128)(2,1)S(1)} collective-permute-done((bf16[1024,256]{0,1:T(8,128)(2,1)S(1)}, bf16[1024,256]{0,1:T(8,128)(2,1)S(1)}, u32[]{:S(2)}, u32[]{:S(2)}) %collective-permute-start.24) | collective-permute-done | bytes 524320 | tf_op jit(solution)/shard_map/ppermute | solution.py:19
  78.5 11.2 %collective-permute-done.29 = bf16[1024,256]{0,1:T(8,128)(2,1)S(1)} collective-permute-done((bf16[1024,256]{0,1:T(8,128)(2,1)S(1)}, bf16[1024,256]{0,1:T(8,128)(2,1)S(1)}, u32[]{:S(2)}, u32[]{:S(2)}) %collective-permute-start.29) | collective-permute-done | bytes 524320 | tf_op jit(solution)/shard_map/ppermute | solution.py:19
  89.8 11.2 %collective-permute-done.10 = bf16[1024,256]{0,1:T(8,128)(2,1)S(1)} collective-permute-done((bf16[1024,256]{0,1:T(8,128)(2,1)S(1)}, bf16[1024,256]{0,1:T(8,128)(2,1)S(1)}, u32[]{:S(2)}, u32[]{:S(2)}) %collective-permute-start.10) | collective-permute-done | bytes 524320 | tf_op jit(solution)/shard_map/ppermute | solution.py:19
  102.3 9.5 %collective-permute-done.17 = bf16[1024,256]{0,1:T(8,128)(2,1)S(1)} collective-permute-done((bf16[1024,256]{0,1:T(8,128)(2,1)S(1)}, bf16[1024,256]{0,1:T(8,128)(2,1)S(1)}, u32[]{:S(2)}, u32[]{:S(2)}) %collective-permute-start.17) | collective-permute-done | bytes 524320 | tf_op jit(solution)/shard_map/ppermute | solution.py:19
  116.4 10.3 %collective-permute-done.12 = bf16[1024,256]{0,1:T(8,128)(2,1)S(1)} collective-permute-done((bf16[1024,256]{0,1:T(8,128)(2,1)S(1)}, bf16[1024,256]{0,1:T(8,128)(2,1)S(1)}, u32[]{:S(2)}, u32[]{:S(2)}) %collective-permute-start.12) | collective-permute-done | bytes 524320 | tf_op jit(solution)/shard_map/ppermute | solution.py:19
  127.7 8.9 %collective-permute-done.19 = bf16[1024,256]{0,1:T(8,128)(2,1)S(1)} collective-permute-done((bf16[1024,256]{0,1:T(8,128)(2,1)S(1)}, bf16[1024,256]{0,1:T(8,128)(2,1)S(1)}, u32[]{:S(2)}, u32[]{:S(2)}) %collective-permute-start.19) | collective-permute-done | bytes 524320 | tf_op jit(solution)/shard_map/ppermute | solution.py:19
  139.1 8.0 %convolution_bitcast_fusion.1 = f32[2,1024,1152]{2,1,0:T(8,128)} fusion(bf16[2,1024,1152]{2,1,0:T(8,128)(2,1)S(1)} %bitcast.314, f32[1024]{0:T(1024)S(1)} %bitcast.370, f32[1024]{0:T(1024)S(1)} %add_rsqrt_fusion.1, bf16[1024,512]{0,1:T(8,128)(2,1)S(1)} %maximum_select_fusion.12, bf16[1024,512]{0,1:T(8,128)(2,1)S(1)} %maximum_select_fusion.13, pred[]{:T(512)S(6)} %eq.25), kind=kOutput, calls=%fused_computation.1 | convolution fusion | flops 4845469696 | bytes 16261121 | tf_op jit(solution)/shard_map/td,kdf->ktf/dot_general | solution.py:194
  147.1 10.3 %add_reduce_fusion.1 = (f32[1024]{0:T(1024)S(1)}, bf16[1024,1152]{1,0:T(8,128)(2,1)}, bf16[1024,1152]{1,0:T(8,128)(2,1)}, bf16[1024,1152]{1,0:T(8,128)(2,1)}) fusion(f32[2,1024,1152]{2,1,0:T(8,128)} %convolution_bitcast_fusion.1, bf16[1152,1024]{1,0:T(8,128)(2,1)S(1)} %copy-done.44, bf16[1024,512]{0,1:T(8,128)(2,1)S(1)} %maximum_select_fusion.17, ...), kind=kOutput, calls=%fused_computation.17 | convolution fusion | flops 2448817152 | bytes 20976640 | tf_op jit(solution)/shard_map/dot_general | solution.py:108
  157.5 7.4 %fusion.91 = f32[1024,1152]{1,0:T(8,128)} fusion(bf16[1024,1152]{1,0:T(8,128)(2,1)} %get-tuple-element.88, bf16[1024,512]{0,1:T(8,128)(2,1)S(1)} %maximum_select_fusion.17, bf16[1024,512]{0,1:T(8,128)(2,1)S(1)} %maximum_select_fusion.16, pred[1024]{0:T(1024)(128)(4,1)S(1)} %get-tuple-element.129, pred[]{:T(512)S(6)} %eq.25), kind=kOutput, calls=%fused_computation.267 | convolution fusion | flops 2426404864 | bytes 9176065 | tf_op jit(solution)/shard_map/dot_general | solution.py:104
  166.4 8.0 %convolution_bitcast_fusion = f32[2,1024,1152]{2,1,0:T(8,128)} fusion(bf16[2,1024,1152]{2,1,0:T(8,128)(2,1)S(1)} %bitcast.314, f32[1024]{0:T(1024)S(1)} %add_rsqrt_fusion, f32[1024]{0:T(1024)S(1)} %bitcast.371, bf16[1024,512]{0,1:T(8,128)(2,1)S(1)} %maximum_select_fusion.14, bf16[1024,512]{0,1:T(8,128)(2,1)S(1)} %maximum_select_fusion.15, pred[]{:T(512)S(6)} %eq.25), kind=kOutput, calls=%fused_computation | convolution fusion | flops 4845469696 | bytes 16261121 | tf_op jit(solution)/shard_map/td,kdf->ktf/dot_general | solution.py:194
  175.9 9.6 %add_reduce_fusion = (f32[1024]{0:T(1024)S(1)}, bf16[1024,1152]{1,0:T(8,128)(2,1)S(1)}, bf16[1024,1152]{1,0:T(8,128)(2,1)}, bf16[1024,1152]{1,0:T(8,128)(2,1)}) fusion(f32[2,1024,1152]{2,1,0:T(8,128)} %convolution_bitcast_fusion, bf16[1152,1024]{1,0:T(8,128)(2,1)S(1)} %copy-done.44, bf16[1024,512]{0,1:T(8,128)(2,1)S(1)} %maximum_select_fusion.19, ...), kind=kOutput, calls=%fused_computation.16 | convolution fusion | flops 2448817152 | bytes 20976640 | tf_op jit(solution)/shard_map/dot_general | solution.py:108
  185.6 4.7 fusion.74
  211.3 3.4 fusion.138
  215.2 3.6 bitcast_convert_fusion.6
  222.4 3.6 bitcast_convert_fusion.5
  226.0 4.0 fusion.32
  248.9 4.9 bitcast_add_fusion.4
  260.3 8.5 %collective-permute-done.63 = bf16[4,128,1152]{2,1,0:T(8,128)(2,1)S(1)} collective-permute-done((bf16[4,128,1152]{2,1,0:T(8,128)(2,1)S(1)}, bf16[4,128,1152]{2,1,0:T(8,128)(2,1)S(1)}, u32[]{:S(2)}, u32[]{:S(2)}) %collective-permute-start.63) | collective-permute-done | bytes 1179680 | tf_op jit(solution)/shard_map/ppermute | solution.py:90
  269.4 24.0 %collective-permute-done.66 = bf16[4,128,1152]{2,1,0:T(8,128)(2,1)S(1)} collective-permute-done((bf16[4,128,1152]{2,1,0:T(8,128)(2,1)S(1)}, bf16[4,128,1152]{2,1,0:T(8,128)(2,1)S(1)}, u32[]{:S(2)}, u32[]{:S(2)}) %collective-permute-start.66) | collective-permute-done | bytes 1179680 | tf_op jit(solution)/shard_map/ppermute | solution.py:90
  306.1 3.9 collective-permute-done.70
  311.2 11.4 %collective-permute-done.64 = bf16[2,128,1152]{2,1,0:T(8,128)(2,1)} collective-permute-done((bf16[2,128,1152]{2,1,0:T(8,128)(2,1)}, bf16[2,128,1152]{2,1,0:T(8,128)(2,1)}, u32[]{:S(2)}, u32[]{:S(2)}) %collective-permute-start.64) | collective-permute-done | bytes 589856 | tf_op jit(solution)/shard_map/ppermute | solution.py:90
  324.1 9.5 %collective-permute-done.67 = bf16[2,128,1152]{2,1,0:T(8,128)(2,1)} collective-permute-done((bf16[2,128,1152]{2,1,0:T(8,128)(2,1)}, bf16[2,128,1152]{2,1,0:T(8,128)(2,1)}, u32[]{:S(2)}, u32[]{:S(2)}) %collective-permute-start.67) | collective-permute-done | bytes 589856 | tf_op jit(solution)/shard_map/ppermute | solution.py:90
  337.4 10.7 %collective-permute-done.71 = bf16[1,128,1152]{2,1,0:T(8,128)(2,1)S(1)} collective-permute-done((bf16[1,128,1152]{2,1,0:T(8,128)(2,1)S(1)}, bf16[1,128,1152]{2,1,0:T(8,128)(2,1)S(1)}, u32[]{:S(2)}, u32[]{:S(2)}) %collective-permute-start.71) | collective-permute-done | bytes 294944 | tf_op jit(solution)/shard_map/ppermute | solution.py:90
  348.2 15.0 %collective-permute-done.65 = bf16[1,128,1152]{2,1,0:T(8,128)(2,1)S(1)} collective-permute-done((bf16[1,128,1152]{2,1,0:T(8,128)(2,1)S(1)}, bf16[1,128,1152]{2,1,0:T(8,128)(2,1)S(1)}, u32[]{:S(2)}, u32[]{:S(2)}) %collective-permute-start.65) | collective-permute-done | bytes 294944 | tf_op jit(solution)/shard_map/ppermute | solution.py:90
  363.3 14.1 %collective-permute-done.68 = bf16[1,128,1152]{2,1,0:T(8,128)(2,1)S(1)} collective-permute-done((bf16[1,128,1152]{2,1,0:T(8,128)(2,1)S(1)}, bf16[1,128,1152]{2,1,0:T(8,128)(2,1)S(1)}, u32[]{:S(2)}, u32[]{:S(2)}) %collective-permute-start.68) | collective-permute-done | bytes 294944 | tf_op jit(solution)/shard_map/ppermute | solution.py:90
  410.2 3.8 reshape.228
  414.1 3.5 constant_dynamic-slice_fusion
  432.9 3.4 copy.98
  467.9 5.9 %collective-permute-done.56 = bf16[1,128,768]{2,1,0:T(8,128)(2,1)} collective-permute-done((bf16[1,128,768]{2,1,0:T(8,128)(2,1)}, bf16[1,128,768]{2,1,0:T(8,128)(2,1)}, u32[]{:S(2)}, u32[]{:S(2)}) %collective-permute-start.56) | collective-permute-done | bytes 196640 | tf_op jit(solution)/shard_map/ppermute | solution.py:90
  474.8 6.3 %collective-permute-done.48 = bf16[1024,256]{0,1:T(8,128)(2,1)S(1)} collective-permute-done((bf16[1024,256]{0,1:T(8,128)(2,1)}, bf16[1024,256]{0,1:T(8,128)(2,1)S(1)}, u32[]{:S(2)}, u32[]{:S(2)}) %collective-permute-start.48) | collective-permute-done | bytes 524320 | tf_op jit(solution)/shard_map/ppermute | solution.py:19
  (615 shorter events, 235.2 us)
Async XLA Ops:
  5.2 23.3 %collective-permute-start.3 = (bf16[1024,256]{0,1:T(8,128)(2,1)S(1)}, bf16[1024,256]{0,1:T(8,128)(2,1)}, u32[]{:S(2)}, u32[]{:S(2)}) collective-permute-start(bf16[1024,256]{0,1:T(8,128)(2,1)S(1)} %copy.136), channel_id=1, source_target_pairs={{0,1},{1,0},{2,3},{3,2},{4,5},{5,4},{6,7},{7,6},{8,9},{9,8},{10,11... | collective-permute-start | bytes 1572872 | tf_op jit(solution)/shard_map/ppermute | solution.py:14
  6.6 21.9 %collective-permute-start.1 = (bf16[1024,256]{0,1:T(8,128)(2,1)S(1)}, bf16[1024,256]{0,1:T(8,128)(2,1)}, u32[]{:S(2)}, u32[]{:S(2)}) collective-permute-start(bf16[1024,256]{0,1:T(8,128)(2,1)S(1)} %copy.133), channel_id=1, source_target_pairs={{0,2},{1,3},{2,0},{3,1},{4,6},{5,7},{6,4},{7,5},{8,10},{9,11},{10,... | collective-permute-start | bytes 1572872 | tf_op jit(solution)/shard_map/ppermute | solution.py:19
  65.5 24.2 %collective-permute-start.29 = (bf16[1024,256]{0,1:T(8,128)(2,1)S(1)}, bf16[1024,256]{0,1:T(8,128)(2,1)S(1)}, u32[]{:S(2)}, u32[]{:S(2)}) collective-permute-start(bf16[1024,256]{0,1:T(8,128)(2,1)S(1)} %copy.135), channel_id=1, source_target_pairs={{0,2},{1,3},{2,0},{3,1},{4,6},{5,7},{6,4},{7,5},{8,10},{9,11},{10,... | collective-permute-start | bytes 1572872 | tf_op jit(solution)/shard_map/ppermute | solution.py:19
  67.6 33.4 %collective-permute-start.10 = (bf16[1024,256]{0,1:T(8,128)(2,1)S(1)}, bf16[1024,256]{0,1:T(8,128)(2,1)S(1)}, u32[]{:S(2)}, u32[]{:S(2)}) collective-permute-start(bf16[1024,256]{0,1:T(8,128)(2,1)S(1)} %slice.562), channel_id=1, source_target_pairs={{0,2},{1,3},{2,0},{3,1},{4,6},{5,7},{6,4},{7,5},{8,10},{9,11},{10,... | collective-permute-start | bytes 1572872 | tf_op jit(solution)/shard_map/ppermute | solution.py:19
  70.0 41.8 %collective-permute-start.17 = (bf16[1024,256]{0,1:T(8,128)(2,1)S(1)}, bf16[1024,256]{0,1:T(8,128)(2,1)S(1)}, u32[]{:S(2)}, u32[]{:S(2)}) collective-permute-start(bf16[1024,256]{0,1:T(8,128)(2,1)S(1)} %slice.560), channel_id=1, source_target_pairs={{0,2},{1,3},{2,0},{3,1},{4,6},{5,7},{6,4},{7,5},{8,10},{9,11},{10,... | collective-permute-start | bytes 1572872 | tf_op jit(solution)/shard_map/ppermute | solution.py:19
  70.4 44.4 %collective-permute-start.23 = (bf16[1024,256]{0,1:T(8,128)(2,1)S(1)}, bf16[1024,256]{0,1:T(8,128)(2,1)S(1)}, u32[]{:S(2)}, u32[]{:S(2)}) collective-permute-start(bf16[1024,256]{0,1:T(8,128)(2,1)S(1)} %copy.134), channel_id=1, source_target_pairs={{0,1},{1,0},{2,3},{3,2},{4,5},{5,4},{6,7},{7,6},{8,9},{9,8},{10,11... | collective-permute-start | bytes 1572872 | tf_op jit(solution)/shard_map/ppermute | solution.py:14
  78.5 36.3 %collective-permute-start.28 = (bf16[1024,256]{0,1:T(8,128)(2,1)S(1)}, bf16[1024,256]{0,1:T(8,128)(2,1)S(1)}, u32[]{:S(2)}, u32[]{:S(2)}) collective-permute-start(bf16[1024,256]{0,1:T(8,128)(2,1)S(1)} %copy.135), channel_id=1, source_target_pairs={{0,1},{1,0},{2,3},{3,2},{4,5},{5,4},{6,7},{7,6},{8,9},{9,8},{10,11... | collective-permute-start | bytes 1572872 | tf_op jit(solution)/shard_map/ppermute | solution.py:14
  89.8 25.9 %collective-permute-start.25 = (bf16[1024,256]{0,1:T(8,128)(2,1)S(1)}, bf16[1024,256]{0,1:T(8,128)(2,1)S(1)}, u32[]{:S(2)}, u32[]{:S(2)}) collective-permute-start(bf16[1024,256]{0,1:T(8,128)(2,1)S(1)} %collective-permute-done.24), channel_id=1, source_target_pairs={{0,1},{1,0},{2,3},{3,2},{4,5},{5,4},{6,7},{7,6},{8,9},{9,8},{10,11... | collective-permute-start | bytes 1572872 | tf_op jit(solution)/shard_map/ppermute | solution.py:14
  101.0 26.2 %collective-permute-start.30 = (bf16[1024,256]{0,1:T(8,128)(2,1)S(1)}, bf16[1024,256]{0,1:T(8,128)(2,1)S(1)}, u32[]{:S(2)}, u32[]{:S(2)}) collective-permute-start(bf16[1024,256]{0,1:T(8,128)(2,1)S(1)} %collective-permute-done.29), channel_id=1, source_target_pairs={{0,1},{1,0},{2,3},{3,2},{4,5},{5,4},{6,7},{7,6},{8,9},{9,8},{10,11... | collective-permute-start | bytes 1572872 | tf_op jit(solution)/shard_map/ppermute | solution.py:14
  114.8 21.8 %collective-permute-start.11 = (bf16[1024,256]{0,1:T(8,128)(2,1)S(1)}, bf16[1024,256]{0,1:T(8,128)(2,1)S(1)}, u32[]{:S(2)}, u32[]{:S(2)}) collective-permute-start(bf16[1024,256]{0,1:T(8,128)(2,1)S(1)} %get-tuple-element.78), channel_id=1, source_target_pairs={{0,1},{1,0},{2,3},{3,2},{4,5},{5,4},{6,7},{7,6},{8,9},{9,8},{10,11... | collective-permute-start | bytes 1572872 | tf_op jit(solution)/shard_map/ppermute | solution.py:14
  114.8 21.8 %collective-permute-start.19 = (bf16[1024,256]{0,1:T(8,128)(2,1)S(1)}, bf16[1024,256]{0,1:T(8,128)(2,1)S(1)}, u32[]{:S(2)}, u32[]{:S(2)}) collective-permute-start(bf16[1024,256]{0,1:T(8,128)(2,1)S(1)} %get-tuple-element.82), channel_id=1, source_target_pairs={{0,2},{1,3},{2,0},{3,1},{4,6},{5,7},{6,4},{7,5},{8,10},{9,11},{10,... | collective-permute-start | bytes 1572872 | tf_op jit(solution)/shard_map/ppermute | solution.py:19
  115.7 21.4 %collective-permute-start.18 = (bf16[1024,256]{0,1:T(8,128)(2,1)S(1)}, bf16[1024,256]{0,1:T(8,128)(2,1)S(1)}, u32[]{:S(2)}, u32[]{:S(2)}) collective-permute-start(bf16[1024,256]{0,1:T(8,128)(2,1)S(1)} %get-tuple-element.82), channel_id=1, source_target_pairs={{0,1},{1,0},{2,3},{3,2},{4,5},{5,4},{6,7},{7,6},{8,9},{9,8},{10,11... | collective-permute-start | bytes 1572872 | tf_op jit(solution)/shard_map/ppermute | solution.py:14
  136.6 28.3 %collective-permute-start.20 = (bf16[1024,256]{0,1:T(8,128)(2,1)S(1)}, bf16[1024,256]{0,1:T(8,128)(2,1)S(1)}, u32[]{:S(2)}, u32[]{:S(2)}) collective-permute-start(bf16[1024,256]{0,1:T(8,128)(2,1)S(1)} %collective-permute-done.19), channel_id=1, source_target_pairs={{0,1},{1,0},{2,3},{3,2},{4,5},{5,4},{6,7},{7,6},{8,9},{9,8},{10,11... | collective-permute-start | bytes 1572872 | tf_op jit(solution)/shard_map/ppermute | solution.py:14
  199.5 57.5 %collective-permute-start.69 = (bf16[4,128,1152]{2,1,0:T(8,128)(2,1)}, bf16[4,128,1152]{2,1,0:T(8,128)(2,1)}, u32[]{:S(2)}, u32[]{:S(2)}) collective-permute-start(bf16[4,128,1152]{2,1,0:T(8,128)(2,1)} %fusion.39), channel_id=1, source_target_pairs={{0,4},{4,0},{8,12},{12,8},{16,20},{20,16},{24,28},{28,24},{1,5},{5... | collective-permute-start | bytes 3538952 | tf_op jit(solution)/shard_map/ppermute | solution.py:90
  214.6 30.6 %collective-permute-start.14 = (bf16[1024,512]{0,1:T(8,128)(2,1)}, bf16[1024,512]{0,1:T(8,128)(2,1)}, u32[]{:S(2)}, u32[]{:S(2)}) collective-permute-start(bf16[1024,512]{0,1:T(8,128)(2,1)} %convolution_convert_fusion.2), channel_id=1, source_target_pairs={{0,1},{1,0},{2,3},{3,2},{4,5},{5,4},{6,7},{7,6},{8,9},{9,8},{10,11... | collective-permute-start | bytes 3145736 | tf_op jit(solution)/shard_map/ppermute | solution.py:14
  218.8 29.5 %collective-permute-start.26 = (bf16[1024,512]{0,1:T(8,128)(2,1)}, bf16[1024,512]{0,1:T(8,128)(2,1)}, u32[]{:S(2)}, u32[]{:S(2)}) collective-permute-start(bf16[1024,512]{0,1:T(8,128)(2,1)} %bitcast_convert_fusion.6), channel_id=1, source_target_pairs={{0,1},{1,0},{2,3},{3,2},{4,5},{5,4},{6,7},{7,6},{8,9},{9,8},{10,11... | collective-permute-start | bytes 3145736 | tf_op jit(solution)/shard_map/ppermute | solution.py:14
  240.0 28.9 %collective-permute-start.63 = (bf16[4,128,1152]{2,1,0:T(8,128)(2,1)S(1)}, bf16[4,128,1152]{2,1,0:T(8,128)(2,1)S(1)}, u32[]{:S(2)}, u32[]{:S(2)}) collective-permute-start(bf16[4,128,1152]{2,1,0:T(8,128)(2,1)S(1)} %fusion.38), channel_id=1, source_target_pairs={{0,4},{4,0},{8,12},{12,8},{16,20},{20,16},{24,28},{28,24},{1,5},{5... | collective-permute-start | bytes 3538952 | tf_op jit(solution)/shard_map/ppermute | solution.py:90
  248.4 45.0 %collective-permute-start.66 = (bf16[4,128,1152]{2,1,0:T(8,128)(2,1)S(1)}, bf16[4,128,1152]{2,1,0:T(8,128)(2,1)S(1)}, u32[]{:S(2)}, u32[]{:S(2)}) collective-permute-start(bf16[4,128,1152]{2,1,0:T(8,128)(2,1)S(1)} %copy-done.52), channel_id=1, source_target_pairs={{0,4},{4,0},{8,12},{12,8},{16,20},{20,16},{24,28},{28,24},{1,5},{5... | collective-permute-start | bytes 3538952 | tf_op jit(solution)/shard_map/ppermute | solution.py:90
  253.9 43.1 %collective-permute-start.15 = (bf16[1024,256]{0,1:T(8,128)(2,1)S(1)}, bf16[1024,256]{0,1:T(8,128)(2,1)S(1)}, u32[]{:S(2)}, u32[]{:S(2)}) collective-permute-start(bf16[1024,256]{0,1:T(8,128)(2,1)S(1)} %slice.561), channel_id=1, source_target_pairs={{0,2},{1,3},{2,0},{3,1},{4,6},{5,7},{6,4},{7,5},{8,10},{9,11},{10,... | collective-permute-start | bytes 1572872 | tf_op jit(solution)/shard_map/ppermute | solution.py:19
  254.9 42.5 %collective-permute-start.27 = (bf16[1024,256]{0,1:T(8,128)(2,1)S(1)}, bf16[1024,256]{0,1:T(8,128)(2,1)S(1)}, u32[]{:S(2)}, u32[]{:S(2)}) collective-permute-start(bf16[1024,256]{0,1:T(8,128)(2,1)S(1)} %slice.558), channel_id=1, source_target_pairs={{0,2},{1,3},{2,0},{3,1},{4,6},{5,7},{6,4},{7,5},{8,10},{9,11},{10,... | collective-permute-start | bytes 1572872 | tf_op jit(solution)/shard_map/ppermute | solution.py:19
  257.0 44.0 %collective-permute-start.22 = (bf16[1024,256]{0,1:T(8,128)(2,1)S(1)}, bf16[1024,256]{0,1:T(8,128)(2,1)S(1)}, u32[]{:S(2)}, u32[]{:S(2)}) collective-permute-start(bf16[1024,256]{0,1:T(8,128)(2,1)S(1)} %slice.559), channel_id=1, source_target_pairs={{0,2},{1,3},{2,0},{3,1},{4,6},{5,7},{6,4},{7,5},{8,10},{9,11},{10,... | collective-permute-start | bytes 1572872 | tf_op jit(solution)/shard_map/ppermute | solution.py:19
  268.8 33.2 %collective-permute-start.37 = (bf16[1024,256]{0,1:T(8,128)(2,1)S(1)}, bf16[1024,256]{0,1:T(8,128)(2,1)S(1)}, u32[]{:S(2)}, u32[]{:S(2)}) collective-permute-start(bf16[1024,256]{0,1:T(8,128)(2,1)S(1)} %slice.557), channel_id=1, source_target_pairs={{0,2},{1,3},{2,0},{3,1},{4,6},{5,7},{6,4},{7,5},{8,10},{9,11},{10,... | collective-permute-start | bytes 1572872 | tf_op jit(solution)/shard_map/ppermute | solution.py:19
  297.0 25.6 %collective-permute-start.64 = (bf16[2,128,1152]{2,1,0:T(8,128)(2,1)}, bf16[2,128,1152]{2,1,0:T(8,128)(2,1)}, u32[]{:S(2)}, u32[]{:S(2)}) collective-permute-start(bf16[2,128,1152]{2,1,0:T(8,128)(2,1)} %fusion.76), channel_id=1, source_target_pairs={{0,8},{4,12},{8,0},{12,4},{16,24},{20,28},{24,16},{28,20},{1,9},{5... | collective-permute-start | bytes 1769480 | tf_op jit(solution)/shard_map/ppermute | solution.py:90
  297.5 36.1 %collective-permute-start.67 = (bf16[2,128,1152]{2,1,0:T(8,128)(2,1)}, bf16[2,128,1152]{2,1,0:T(8,128)(2,1)}, u32[]{:S(2)}, u32[]{:S(2)}) collective-permute-start(bf16[2,128,1152]{2,1,0:T(8,128)(2,1)} %fusion.78), channel_id=1, source_target_pairs={{0,8},{4,12},{8,0},{12,4},{16,24},{20,28},{24,16},{28,20},{1,9},{5... | collective-permute-start | bytes 1769480 | tf_op jit(solution)/shard_map/ppermute | solution.py:90
  301.0 79.1 %collective-permute-start.33 = (bf16[1024,256]{0,1:T(8,128)(2,1)}, bf16[1024,256]{0,1:T(8,128)(2,1)}, u32[]{:S(2)}, u32[]{:S(2)}) collective-permute-start(bf16[1024,256]{0,1:T(8,128)(2,1)} %get-tuple-element.70), channel_id=1, source_target_pairs={{0,1},{1,0},{2,3},{3,2},{4,5},{5,4},{6,7},{7,6},{8,9},{9,8},{10,11... | collective-permute-start | bytes 1572872 | tf_op jit(solution)/shard_map/ppermute | solution.py:14
  302.0 76.5 %collective-permute-start.34 = (bf16[1024,256]{0,1:T(8,128)(2,1)}, bf16[1024,256]{0,1:T(8,128)(2,1)}, u32[]{:S(2)}, u32[]{:S(2)}) collective-permute-start(bf16[1024,256]{0,1:T(8,128)(2,1)} %get-tuple-element.70), channel_id=1, source_target_pairs={{0,2},{1,3},{2,0},{3,1},{4,6},{5,7},{6,4},{7,5},{8,10},{9,11},{10,... | collective-permute-start | bytes 1572872 | tf_op jit(solution)/shard_map/ppermute | solution.py:19
  310.0 72.1 %collective-permute-start.40 = (bf16[1024,256]{0,1:T(8,128)(2,1)}, bf16[1024,256]{0,1:T(8,128)(2,1)S(1)}, u32[]{:S(2)}, u32[]{:S(2)}) collective-permute-start(bf16[1024,256]{0,1:T(8,128)(2,1)} %get-tuple-element.74), channel_id=1, source_target_pairs={{0,1},{1,0},{2,3},{3,2},{4,5},{5,4},{6,7},{7,6},{8,9},{9,8},{10,11... | collective-permute-start | bytes 1572872 | tf_op jit(solution)/shard_map/ppermute | solution.py:14
  322.6 57.0 %collective-permute-start.41 = (bf16[1024,256]{0,1:T(8,128)(2,1)S(1)}, bf16[1024,256]{0,1:T(8,128)(2,1)S(1)}, u32[]{:S(2)}, u32[]{:S(2)}) collective-permute-start(bf16[1024,256]{0,1:T(8,128)(2,1)S(1)} %copy-done.45), channel_id=1, source_target_pairs={{0,2},{1,3},{2,0},{3,1},{4,6},{5,7},{6,4},{7,5},{8,10},{9,11},{10,... | collective-permute-start | bytes 1572872 | tf_op jit(solution)/shard_map/ppermute | solution.py:19
  394.2 50.2 %collective-permute-start.60 = (bf16[4,128,256]{2,1,0:T(8,128)(2,1)}, bf16[4,128,256]{2,1,0:T(8,128)(2,1)}, u32[]{:S(2)}, u32[]{:S(2)}) collective-permute-start(bf16[4,128,256]{2,1,0:T(8,128)(2,1)} %fusion.84), channel_id=1, source_target_pairs={{0,4},{4,0},{8,12},{12,8},{16,20},{20,16},{24,28},{28,24},{1,5},{5... | collective-permute-start | bytes 786440 | tf_op jit(solution)/shard_map/ppermute | solution.py:90
  396.4 33.8 %collective-permute-start.57 = (f32[4,256]{1,0:T(4,128)}, f32[4,256]{1,0:T(4,128)}, u32[]{:S(2)}, u32[]{:S(2)}) collective-permute-start(f32[4,256]{1,0:T(4,128)} %pad_maximum_fusion.53), channel_id=1, source_target_pairs={{0,4},{4,0},{8,12},{12,8},{16,20},{20,16},{24,28},{28,24},{1,5},{5... | collective-permute-start | bytes 12296 | tf_op jit(solution)/shard_map/ppermute | solution.py:75
  420.5 33.9 %collective-permute-start.54 = (bf16[4,128,768]{2,1,0:T(8,128)(2,1)}, bf16[4,128,768]{2,1,0:T(8,128)(2,1)}, u32[]{:S(2)}, u32[]{:S(2)}) collective-permute-start(bf16[4,128,768]{2,1,0:T(8,128)(2,1)} %bitcast.260), channel_id=1, source_target_pairs={{0,4},{4,0},{8,12},{12,8},{16,20},{20,16},{24,28},{28,24},{1,5},{5... | collective-permute-start | bytes 2359304 | tf_op jit(solution)/shard_map/ppermute | solution.py:90
  439.2 21.4 %collective-permute-start.47 = (bf16[1024,512]{0,1:T(8,128)(2,1)}, bf16[1024,512]{0,1:T(8,128)(2,1)S(1)}, u32[]{:S(2)}, u32[]{:S(2)}) collective-permute-start(bf16[1024,512]{0,1:T(8,128)(2,1)} %bitcast_convert_fusion.3), channel_id=1, source_target_pairs={{0,1},{1,0},{2,3},{3,2},{4,5},{5,4},{6,7},{7,6},{8,9},{9,8},{10,11... | collective-permute-start | bytes 3145736 | tf_op jit(solution)/shard_map/ppermute | solution.py:14
  (189 other events, 2218.6 us)

commit v3 on v2

--- a/solution.py
+++ b/solution.py
@@ -27,8 +27,10 @@
     )
 
 
-def gather_columns(values, core, chip):
-    from_chip = swap_chip(values)
+def gather_columns(values, core, chip, *others, fetched=None):
+    from_chip = swap_chip(values) if fetched is None else fetched
+    if others:
+        from_chip = after(from_chip, *others)
     from_core = swap_core(values)
     from_both = swap_core(from_chip)
     near = ordered(core == 0, values, from_core)
@@ -77,19 +79,25 @@
     return values
 
 
-def scatter_groups(values):
+def scatter_groups(values, swapped=False, holds=()):
     size = lax.axis_size("dp")
     index = lax.axis_index("dp")
     block = values.shape[0] // size
-    step = 1
-    while step < size:
-        pairs = values.reshape(-1, 2, block, values.shape[-1])
+    left = [step for step in (1 << bit for bit in range(size.bit_length() - 1))]
+    order = list(left)
+    if swapped:
+        order[:2] = order[:2][::-1]
+    for place, step in enumerate(order):
+        lower = 1 << left.index(step)
+        left.remove(step)
+        pairs = values.reshape(-1, 2, lower * block, values.shape[-1])
         bit = (index // step) % 2
         sent = lax.dynamic_index_in_dim(pairs, 1 - bit, 1, keepdims=False).astype(BF16)
         kept = lax.dynamic_index_in_dim(pairs, bit, 1, keepdims=False)
         moved = lax.ppermute(sent, "dp", [(i, i ^ step) for i in range(size)])
+        if place < len(holds):
+            moved = after(moved, *holds[place])
         values = kept + moved.astype(F32)
-        step *= 2
     return values.reshape(block, -1)
 
 
@@ -146,9 +154,11 @@
 
     gains = gather_columns(jnp.stack([gain_one, gain_two]), core, chip).astype(F32)
     gain_one_full, gain_two_full = gains[0:1], gains[1:2]
-    token_full = [gather_columns(part, core, chip) for part in token_parts]
-    held = lax.optimization_barrier(tuple(grad_parts) + tuple(token_full))
-    grad_later, token_full = held[:CHUNKS], held[CHUNKS:]
+    token_far = [swap_chip(part) for part in token_parts]
+    token_full = [
+        gather_columns(part, core, chip, fetched=far) for part, far in zip(token_parts, token_far)
+    ]
+    grad_far = [swap_chip(after(part, far)) for part, far in zip(grad_parts, token_far)]
 
     out_sent, out_kept = split_columns(weight_out, 1, core, chip)
     down_sent, down_kept = split_columns(weight_down, 1, core, chip)
@@ -179,15 +189,19 @@
                 jnp.dot(mixer_rows[k], out_kept, preferred_element_type=F32),
             )
         )
+    mixer_parts = [(sent, after(kept, *grad_far)) for sent, kept in mixer_parts]
     for k, mixer_out in enumerate(scatter_all(mixer_parts)):
         middle.append(token_parts[k].astype(F32) + live[k] * mixer_out)
-        middle_full.append(gather_columns(middle[k].astype(BF16), core, chip))
-
-    grad_full = [gather_columns(part, core, chip) for part in grad_later]
+
+    grad_full = [
+        gather_columns(part, core, chip, fetched=far) for part, far in zip(grad_parts, grad_far)
+    ]
     normed_two, hidden, feed_grad, gu_grad, block_out = [], [], [], [], []
     middle_grad, mixer_grad, gain_two_parts = [], [], []
     scale_two, inner_two, feed_parts = [], [], []
     for k in span:
+        earlier = [kept for sent, kept in feed_parts]
+        middle_full.append(gather_columns(middle[k].astype(BF16), core, chip, *earlier))
         wide = middle_full[k].astype(F32)
         scale = lax.rsqrt(jnp.mean(wide * wide, axis=1, keepdims=True) + EPSILON)
         normed_two.append((wide * scale * gain_two_full).astype(BF16))
@@ -231,8 +245,6 @@
         )
         for k in span
     ]
-    down_shard = scatter_groups(grad_down)
-    feed_shard = [scatter_groups(part) for part in grad_feed]
     mixer_grad = [after(mixer_grad[0], grad_down)] + [
         after(part, *grad_feed, *[kept for sent, kept in down_parts]) for part in mixer_grad[1:]
     ]
@@ -283,6 +295,11 @@
         total_of([dot_rows(normed_one[k], gates_grad[k][side]) for k in span]) for side in range(3)
     ]
     in_shard = scatter_groups(jnp.concatenate(grad_in, axis=1))
+    holds = ((conv_grad[0],), (gates_grad[0],))
+    down_shard = scatter_groups(grad_down, False, holds)
+    feed_shard = [
+        scatter_groups(part, swapped, holds) for part, swapped in zip(grad_feed, (True, False))
+    ]
     for k, normed_grad in enumerate(scatter_all(in_parts, *grad_in)):
         unit = token_parts[k].astype(F32) * scale_one[k]
         gain_one_parts.append(jnp.sum(normed_grad * unit, axis=0))

time: 506 us -> 458 us (0.905)
  local copies, waits for them, and re-layouts: 71.9 us -> 51.1 us
  waiting for transfers between devices: 196 us -> 176 us
  other arithmetic: 61.1 us -> 47.1 us
  matrix products: 113 us -> 121 us
    ppermute x15, waiting for transfers between devices: 105 us -> 65 us  [scatter_groups(): moved = lax.ppermute(sent, 'dp', [(i, i ^ step) for i in range(size)])]
    ppermute x21, waiting for transfers between devices: 83 us -> 99.6 us  [swap_chip(): return lax.ppermute(values, 'tensor', [(i, i ^ 2) for i in range(size)])]
    dot_general x14, matrix products: 30 us -> 44.6 us  [dot_rows(): lax.dot_general(left, right, (((0,), (0,)), ((), ())), preferred_element_...]
    unnamed x301 -> x233, local copies, waits for them, and re-layouts: 22.4 us -> 11.4 us
    dot_general x4 -> x0, local copies, waits for them, and re-layouts: 9.08 us -> none  [the longest x2 4.75 us: body(): jnp.dot(hidden[k], down_kept, preferred_element_type=F32)]
    select_n x22 -> x20, other arithmetic: 18.8 us -> 15 us  [ordered(): jnp.where(is_first, jnp.concatenate([own, other], axis=-1), jnp.concatena...]
  transfers between devices with their start and end apart: 72 -> 72, of which waited for: 28 -> 24; matrix products, arithmetic and copies ran while one was open for 35% -> 46% of each run, Pallas kernels for 0% -> 0%
where the time goes in v3:
time: 458 us; the launch traced here: 453 us
  waiting for transfers between devices  176 us (38%)
  matrix products  121 us (26%)
  starting transfers between devices  54.6 us (12%)
  local copies, waits for them, and re-layouts  51.1 us (11%)
  other arithmetic  47.1 us (10%)
    ppermute x21, waiting for transfers between devices, swap_chip(): return lax.ppermute(values, 'tensor', [(i, i ^ 2) for i in range(size)])  99.6 us
    ppermute x15, waiting for transfers between devices, scatter_groups(): moved = lax.ppermute(sent, 'dp', [(i, i ^ step) for i in range(size)])  65 us
    dot_general x14, matrix products, dot_rows(): lax.dot_general(left, right, (((0,), (0,)), ((), ())), preferred_element_...  44.6 us
    ppermute x21, starting transfers between devices, swap_chip(): return lax.ppermute(values, 'tensor', [(i, i ^ 2) for i in range(size)])  24.9 us
    dot_general x4, matrix products, dot_last(): lax.dot_general(left, right, (((1,), (1,)), ((), ())), preferred_element_...  22.2 us
    ppermute x15, starting transfers between devices, scatter_groups(): moved = lax.ppermute(sent, 'dp', [(i, i ^ step) for i in range(size)])  16.5 us
    dot_general x2, matrix products, body(): jnp.einsum('td,kdf->ktf', normed_two[k], weight_feed, preferred_element_t...  16.4 us
    select_n x20, other arithmetic, ordered(): jnp.where(is_first, jnp.concatenate([own, other], axis=-1), jnp.concatena...  15 us
  transfers between devices with their start and end apart: 72, of which 24 were waited for; matrix products, arithmetic and copies ran while one was open for 46% of the time, Pallas kernels for 0%

profile of v3, /device:TPU:0, one launch (start us, length us, event | category | flops | bytes accessed | tf_op | source)
XLA Modules:
  0.0 452.8 jit_solution(5266566821122147559)
XLA Ops:
  2.1 3.0 collective-permute-start.7
  10.2 7.7 %collective-permute-done.4 = bf16[2,256]{1,0:T(2,128)(2,1)S(1)} collective-permute-done((bf16[2,256]{1,0:T(2,128)(2,1)S(1)}, bf16[2,256]{1,0:T(2,128)(2,1)S(1)}, u32[]{:S(2)}, u32[]{:S(2)}) %collective-permute-start.4) | collective-permute-done | bytes 1056 | tf_op jit(solution)/shard_map/ppermute | solution.py:19
  20.4 7.8 %collective-permute-done.1 = bf16[1024,256]{1,0:T(8,128)(2,1)S(1)} collective-permute-done((bf16[1024,256]{1,0:T(8,128)(2,1)S(1)}, bf16[1024,256]{1,0:T(8,128)(2,1)S(1)}, u32[]{:S(2)}, u32[]{:S(2)}) %collective-permute-start.1) | collective-permute-done | bytes 524320 | tf_op jit(solution)/shard_map/ppermute | solution.py:19
  47.8 11.4 %collective-permute-done.6 = bf16[1024,256]{1,0:T(8,128)(2,1)} collective-permute-done((bf16[1024,256]{1,0:T(8,128)(2,1)}, bf16[1024,256]{1,0:T(8,128)(2,1)}, u32[]{:S(2)}, u32[]{:S(2)}) %collective-permute-start.6) | collective-permute-done | bytes 524320 | tf_op jit(solution)/shard_map/ppermute | solution.py:19
  59.2 10.4 %collective-permute-done.8 = bf16[1024,256]{1,0:T(8,128)(2,1)S(1)} collective-permute-done((bf16[1024,256]{1,0:T(8,128)(2,1)}, bf16[1024,256]{1,0:T(8,128)(2,1)S(1)}, u32[]{:S(2)}, u32[]{:S(2)}) %collective-permute-start.8) | collective-permute-done | bytes 524320 | tf_op jit(solution)/shard_map/ppermute | solution.py:19
  75.4 19.6 %collective-permute-done.10 = bf16[1024,256]{1,0:T(8,128)(2,1)S(1)} collective-permute-done((bf16[1024,256]{1,0:T(8,128)(2,1)S(1)}, bf16[1024,256]{1,0:T(8,128)(2,1)S(1)}, u32[]{:S(2)}, u32[]{:S(2)}) %collective-permute-start.10) | collective-permute-done | bytes 524320 | tf_op jit(solution)/shard_map/ppermute | solution.py:19
  115.6 8.4 %convolution_bitcast_fusion.1 = f32[2,1024,1152]{2,1,0:T(8,128)} fusion(bf16[2,1024,1152]{2,1,0:T(8,128)(2,1)S(1)} %bitcast.317, f32[1024]{0:T(1024)S(1)} %bitcast.367, f32[1024]{0:T(1024)S(1)} %add_rsqrt_fusion.1, bf16[1024,512]{1,0:T(8,128)(2,1)S(1)} %maximum_select_fusion.12, bf16[1024,512]{1,0:T(8,128)(2,1)S(1)} %maximum_select_fusion.13, pred[]{:T(512)S(6)} %eq.25), kind=kOutput, calls=%fused_computation.1 | convolution fusion | flops 4845469696 | bytes 16261121 | tf_op jit(solution)/shard_map/td,kdf->ktf/dot_general | solution.py:208
  124.0 9.3 %add_reduce_fusion.1 = (f32[1024]{0:T(1024)S(1)}, bf16[1024,1152]{1,0:T(8,128)(2,1)S(1)}, bf16[1024,1152]{1,0:T(8,128)(2,1)}, bf16[1024,1152]{1,0:T(8,128)(2,1)}) fusion(f32[2,1024,1152]{2,1,0:T(8,128)} %convolution_bitcast_fusion.1, bf16[1152,1024]{1,0:T(8,128)(2,1)S(1)} %copy-done.35, bf16[1024,512]{1,0:T(8,128)(2,1)S(1)} %maximum_select_fusion.16, ...), kind=kOutput, calls=%fused_computation.17 | convolution fusion | flops 2448817152 | bytes 20976640 | tf_op jit(solution)/shard_map/dot_general | solution.py:116
  133.3 7.9 %fusion.120 = f32[1024,1152]{1,0:T(8,128)} fusion(bf16[1024,1152]{1,0:T(8,128)(2,1)} %get-tuple-element.94, f32[1024]{0:T(1024)S(1)} %bitcast.368, f32[1024]{0:T(1024)S(1)} %add_rsqrt_fusion.1, bf16[1024,512]{1,0:T(8,128)(2,1)S(1)} %maximum_select_fusion.12, bf16[1024,512]{1,0:T(8,128)(2,1)S(1)} %maximum_select_fusion.13, pred[]{:T(512)S(6)} %eq.25), kind=kOutput, calls=%fused_computation.333 | convolution fusion | flops 2429550592 | bytes 9183233 | tf_op jit(solution)/shard_map/dot_general | solution.py:112
  146.3 5.5 %fusion.42 = f32[1024,1152]{1,0:T(8,128)} fusion(bf16[1024,1152]{1,0:T(8,128)(2,1)S(1)} %get-tuple-element.80, f32[1024]{0:T(1024)S(1)} %bitcast.369, f32[1024]{0:T(1024)S(1)} %add_rsqrt_fusion.1, bf16[1024,512]{1,0:T(8,128)(2,1)S(1)} %maximum_select_fusion.12, bf16[1024,512]{1,0:T(8,128)(2,1)S(1)} %maximum_select_fusion.13, pred[]{:T(512)S(6)} %eq.25), kind=kOutput, calls=%fused_computation.122 | convolution fusion | flops 2429550592 | bytes 9183233 | tf_op jit(solution)/shard_map/dot_general | solution.py:112
  151.9 5.4 %fusion.113 = f32[1024,1152]{1,0:T(8,128)} fusion(bf16[1024,1152]{1,0:T(8,128)(2,1)S(1)} %copy-done.109, bf16[1024,512]{1,0:T(8,128)(2,1)S(1)} %maximum_select_fusion.16, bf16[1024,512]{1,0:T(8,128)(2,1)S(1)} %maximum_select_fusion.15, pred[1024]{0:T(1024)(128)(4,1)S(1)} %get-tuple-element.137, pred[]{:T(512)S(6)} %eq.25), kind=kOutput, calls=%fused_computation.331 | convolution fusion | flops 2426404864 | bytes 9176065 | tf_op jit(solution)/shard_map/dot_general | solution.py:112
  168.3 8.0 %convolution_bitcast_fusion = f32[2,1024,1152]{2,1,0:T(8,128)} fusion(bf16[2,1024,1152]{2,1,0:T(8,128)(2,1)S(1)} %bitcast.317, f32[1024]{0:T(1024)S(1)} %add_rsqrt_fusion, f32[1024]{0:T(1024)S(1)} %bitcast.370, bf16[1024,512]{1,0:T(8,128)(2,1)S(1)} %maximum_select_fusion.14, bf16[1024,512]{1,0:T(8,128)(2,1)S(1)} %maximum_select_fusion.17, pred[]{:T(512)S(6)} %eq.25), kind=kOutput, calls=%fused_computation | convolution fusion | flops 4845469696 | bytes 16261121 | tf_op jit(solution)/shard_map/td,kdf->ktf/dot_general | solution.py:208
  176.4 9.8 %add_reduce_fusion = (f32[1024]{0:T(1024)S(1)}, bf16[1024,1152]{1,0:T(8,128)(2,1)S(1)}, bf16[1024,1152]{1,0:T(8,128)(2,1)}, bf16[1024,1152]{1,0:T(8,128)(2,1)}) fusion(f32[2,1024,1152]{2,1,0:T(8,128)} %convolution_bitcast_fusion, bf16[1152,1024]{1,0:T(8,128)(2,1)S(1)} %copy-done.35, bf16[1024,512]{1,0:T(8,128)(2,1)S(1)} %copy-done.53, ...), kind=kOutput, calls=%fused_computation.16 | convolution fusion | flops 2448817152 | bytes 20976640 | tf_op jit(solution)/shard_map/dot_general | solution.py:116
  186.1 4.1 convolution_convert_fusion
  190.2 5.7 %convolution_add_fusion.2 = f32[1024,1152]{1,0:T(8,128)S(1)} fusion(f32[1024,1152]{1,0:T(8,128)} %fusion.113, bf16[1024,1152]{1,0:T(8,128)(2,1)S(1)} %copy-done.110, bf16[1024,512]{1,0:T(8,128)(2,1)S(1)} %copy-done.53, bf16[1024,512]{1,0:T(8,128)(2,1)S(1)} %maximum_select_fusion.18, pred[1024]{0:T(1024)(128)(4,1)S(1)} %get-tuple-element.136, pred[]{:T(512)S(6)} %eq.25), kind=kOutput, calls=%fused_computation.28 | convolution fusion | flops 2427584512 | bytes 13894657 | tf_op jit(solution)/shard_map/dot_general | solution.py:112
  200.9 5.8 %convolution_add_fusion = f32[1024,1152]{1,0:T(8,128)S(1)} fusion(f32[1024,1152]{1,0:T(8,128)} %fusion.120, bf16[1024,1152]{1,0:T(8,128)(2,1)S(1)} %copy-done.105, f32[1024]{0:T(1024)S(1)} %add_rsqrt_fusion, f32[1024]{0:T(1024)S(1)} %bitcast.371, bf16[1024,512]{1,0:T(8,128)(2,1)S(1)} %maximum_select_fusion.14, ...), kind=kOutput, calls=%fused_computation.26 | convolution fusion | flops 2430730240 | bytes 13901825 | tf_op jit(solution)/shard_map/dot_general | solution.py:112
  206.7 5.9 %convolution_add_fusion.1 = f32[1024,1152]{1,0:T(8,128)S(1)} fusion(f32[1024,1152]{1,0:T(8,128)} %fusion.42, bf16[1024,1152]{1,0:T(8,128)(2,1)S(1)} %copy-done.104, f32[1024]{0:T(1024)S(1)} %add_rsqrt_fusion, f32[1024]{0:T(1024)S(1)} %bitcast.372, bf16[1024,512]{1,0:T(8,128)(2,1)S(1)} %maximum_select_fusion.14, ...), kind=kOutput, calls=%fused_computation.27 | convolution fusion | flops 2430730240 | bytes 13901825 | tf_op jit(solution)/shard_map/dot_general | solution.py:112
  212.7 3.2 convert_add_fusion.3
  215.9 5.2 %convert_add_fusion.1 = f32[1024,512]{1,0:T(8,128)S(1)} fusion(bf16[1024,512]{1,0:T(8,128)(2,1)S(1)} %collective-permute-done.36, bf16[2,256,1152]{2,1,0:T(8,128)(2,1)S(1)} %copy-done.45, bf16[2,256,1152]{2,1,0:T(8,128)(2,1)S(1)} %copy-done.46, bf16[1,1024,1152]{2,1,0:T(8,128)(2,1)} %bitcast.378, bf16[1,1024,1152]{2,1,0:T(8,128)(2,1)} %bitcast.377), kind=kOutput, calls=%fused_computation.76 | convolution fusion | flops 2424045568 | bytes 10223616 | tf_op jit(solution)/shard_map/ktf,kdf->td/dot_general | solution.py:224
  228.6 32.2 %collective-permute-done.39 = f32[1024]{0:T(1024)S(1)} collective-permute-done((f32[1024]{0:T(1024)S(1)}, f32[1024]{0:T(1024)S(1)}, u32[]{:S(2)}, u32[]{:S(2)}) %collective-permute-start.39) | collective-permute-done | bytes 4128 | tf_op jit(solution)/shard_map/ppermute | solution.py:19
  274.5 15.2 %collective-permute-done.63 = bf16[2,256,1152]{2,1,0:T(8,128)(2,1)S(1)} collective-permute-done((bf16[2,256,1152]{2,1,0:T(8,128)(2,1)S(1)}, bf16[2,256,1152]{2,1,0:T(8,128)(2,1)S(1)}, u32[]{:S(2)}, u32[]{:S(2)}) %collective-permute-start.63) | collective-permute-done | bytes 1179680 | tf_op jit(solution)/shard_map/ppermute | solution.py:97
  313.1 3.8 reshape.228
  316.9 3.5 constant_dynamic-slice_fusion
  331.1 2.9 copy.37
  334.0 5.3 %copy.28 = f32[4,1,128,768]{3,2,0,1:T(8,128)} copy(f32[4,1,128,768]{2,1,0,3:T(1,128)} %constant_dynamic-slice_fusion.1) | data formatting | bytes 3145728 | tf_op jit(solution)/shard_map/jit(dynamic_index_in_dim)/dynamic_slice | solution.py:96
  357.9 3.3 collective-permute-start.71
  361.6 20.0 %collective-permute-done.71 = bf16[1,128,1152]{2,1,0:T(8,128)(2,1)S(1)} collective-permute-done((bf16[1,128,1152]{2,1,0:T(8,128)(2,1)S(1)}, bf16[1,128,1152]{2,1,0:T(8,128)(2,1)S(1)}, u32[]{:S(2)}, u32[]{:S(2)}) %collective-permute-start.71) | collective-permute-done | bytes 294944 | tf_op jit(solution)/shard_map/ppermute | solution.py:97
  381.7 12.6 %collective-permute-done.65 = bf16[1,128,1152]{2,1,0:T(8,128)(2,1)S(1)} collective-permute-done((bf16[1,128,1152]{2,1,0:T(8,128)(2,1)S(1)}, bf16[1,128,1152]{2,1,0:T(8,128)(2,1)S(1)}, u32[]{:S(2)}, u32[]{:S(2)}) %collective-permute-start.65) | collective-permute-done | bytes 294944 | tf_op jit(solution)/shard_map/ppermute | solution.py:97
  394.6 5.6 %collective-permute-done.68 = bf16[1,128,1152]{2,1,0:T(8,128)(2,1)S(1)} collective-permute-done((bf16[1,128,1152]{2,1,0:T(8,128)(2,1)S(1)}, bf16[1,128,1152]{2,1,0:T(8,128)(2,1)S(1)}, u32[]{:S(2)}, u32[]{:S(2)}) %collective-permute-start.68) | collective-permute-done | bytes 294944 | tf_op jit(solution)/shard_map/ppermute | solution.py:97
  422.9 10.4 %collective-permute-done.56 = bf16[1,128,768]{2,1,0:T(8,128)(2,1)S(1)} collective-permute-done((bf16[1,128,768]{2,1,0:T(8,128)(2,1)}, bf16[1,128,768]{2,1,0:T(8,128)(2,1)S(1)}, u32[]{:S(2)}, u32[]{:S(2)}) %collective-permute-start.56) | collective-permute-done | bytes 196640 | tf_op jit(solution)/shard_map/ppermute | solution.py:97
  434.4 3.3 collective-permute-done.48
  448.8 3.0 collective-permute-done.53
  (534 shorter events, 184.4 us)
Async XLA Ops:
  5.1 23.2 %collective-permute-start.11 = (bf16[1024,256]{1,0:T(8,128)(2,1)S(1)}, bf16[1024,256]{1,0:T(8,128)(2,1)}, u32[]{:S(2)}, u32[]{:S(2)}) collective-permute-start(bf16[1024,256]{1,0:T(8,128)(2,1)S(1)} %get-tuple-element.128), channel_id=1, source_target_pairs={{0,1},{1,0},{2,3},{3,2},{4,5},{5,4},{6,7},{7,6},{8,9},{9,8},{10,11... | collective-permute-start | bytes 1572872 | tf_op jit(solution)/shard_map/ppermute | solution.py:14
  5.8 22.5 %collective-permute-start.1 = (bf16[1024,256]{1,0:T(8,128)(2,1)S(1)}, bf16[1024,256]{1,0:T(8,128)(2,1)S(1)}, u32[]{:S(2)}, u32[]{:S(2)}) collective-permute-start(bf16[1024,256]{1,0:T(8,128)(2,1)S(1)} %get-tuple-element.127), channel_id=1, source_target_pairs={{0,2},{1,3},{2,0},{3,1},{4,6},{5,7},{6,4},{7,5},{8,10},{9,11},{10,... | collective-permute-start | bytes 1572872 | tf_op jit(solution)/shard_map/ppermute | solution.py:19
  19.8 82.0 %collective-permute-start.22 = (bf16[1024,256]{1,0:T(8,128)(2,1)}, bf16[1024,256]{1,0:T(8,128)(2,1)}, u32[]{:S(2)}, u32[]{:S(2)}) collective-permute-start(bf16[1024,256]{1,0:T(8,128)(2,1)} %get-tuple-element.27), channel_id=1, source_target_pairs={{0,1},{1,0},{2,3},{3,2},{4,5},{5,4},{6,7},{7,6},{8,9},{9,8},{10,11... | collective-permute-start | bytes 1572872 | tf_op jit(solution)/shard_map/ppermute | solution.py:14
  41.5 28.6 %collective-permute-start.18 = (bf16[1024,512]{1,0:T(8,128)(2,1)S(1)}, bf16[1024,512]{1,0:T(8,128)(2,1)S(1)}, u32[]{:S(2)}, u32[]{:S(2)}) collective-permute-start(bf16[1024,512]{1,0:T(8,128)(2,1)S(1)} %convolution_convert_fusion.1), channel_id=1, source_target_pairs={{0,1},{1,0},{2,3},{3,2},{4,5},{5,4},{6,7},{7,6},{8,9},{9,8},{10,11... | collective-permute-start | bytes 3145736 | tf_op jit(solution)/shard_map/ppermute | solution.py:14
  45.9 23.8 %collective-permute-start.8 = (bf16[1024,256]{1,0:T(8,128)(2,1)}, bf16[1024,256]{1,0:T(8,128)(2,1)S(1)}, u32[]{:S(2)}, u32[]{:S(2)}) collective-permute-start(bf16[1024,256]{1,0:T(8,128)(2,1)} %get-tuple-element.28), channel_id=1, source_target_pairs={{0,2},{1,3},{2,0},{3,1},{4,6},{5,7},{6,4},{7,5},{8,10},{9,11},{10,... | collective-permute-start | bytes 1572872 | tf_op jit(solution)/shard_map/ppermute | solution.py:19
  46.6 25.8 %collective-permute-start.9 = (bf16[1024,512]{1,0:T(8,128)(2,1)S(1)}, bf16[1024,512]{1,0:T(8,128)(2,1)S(1)}, u32[]{:S(2)}, u32[]{:S(2)}) collective-permute-start(bf16[1024,512]{1,0:T(8,128)(2,1)S(1)} %convolution_convert_fusion.3), channel_id=1, source_target_pairs={{0,1},{1,0},{2,3},{3,2},{4,5},{5,4},{6,7},{7,6},{8,9},{9,8},{10,11... | collective-permute-start | bytes 3145736 | tf_op jit(solution)/shard_map/ppermute | solution.py:14
  59.2 45.0 %collective-permute-start.29 = (bf16[1024,256]{1,0:T(8,128)(2,1)}, bf16[1024,256]{1,0:T(8,128)(2,1)}, u32[]{:S(2)}, u32[]{:S(2)}) collective-permute-start(bf16[1024,256]{1,0:T(8,128)(2,1)} %get-tuple-element.28), channel_id=1, source_target_pairs={{0,1},{1,0},{2,3},{3,2},{4,5},{5,4},{6,7},{7,6},{8,9},{9,8},{10,11... | collective-permute-start | bytes 1572872 | tf_op jit(solution)/shard_map/ppermute | solution.py:14
  70.5 24.5 %collective-permute-start.19 = (bf16[1024,256]{1,0:T(8,128)(2,1)S(1)}, bf16[1024,256]{1,0:T(8,128)(2,1)S(1)}, u32[]{:S(2)}, u32[]{:S(2)}) collective-permute-start(bf16[1024,256]{1,0:T(8,128)(2,1)S(1)} %slice.568), channel_id=1, source_target_pairs={{0,2},{1,3},{2,0},{3,1},{4,6},{5,7},{6,4},{7,5},{8,10},{9,11},{10,... | collective-permute-start | bytes 1572872 | tf_op jit(solution)/shard_map/ppermute | solution.py:19
  72.8 22.3 %collective-permute-start.10 = (bf16[1024,256]{1,0:T(8,128)(2,1)S(1)}, bf16[1024,256]{1,0:T(8,128)(2,1)S(1)}, u32[]{:S(2)}, u32[]{:S(2)}) collective-permute-start(bf16[1024,256]{1,0:T(8,128)(2,1)S(1)} %slice.570), channel_id=1, source_target_pairs={{0,2},{1,3},{2,0},{3,1},{4,6},{5,7},{6,4},{7,5},{8,10},{9,11},{10,... | collective-permute-start | bytes 1572872 | tf_op jit(solution)/shard_map/ppermute | solution.py:19
  75.4 32.6 %collective-permute-start.23 = (bf16[1024,256]{1,0:T(8,128)(2,1)}, bf16[1024,256]{1,0:T(8,128)(2,1)}, u32[]{:S(2)}, u32[]{:S(2)}) collective-permute-start(bf16[1024,256]{1,0:T(8,128)(2,1)} %collective-permute-done.6), channel_id=1, source_target_pairs={{0,1},{1,0},{2,3},{3,2},{4,5},{5,4},{6,7},{7,6},{8,9},{9,8},{10,11... | collective-permute-start | bytes 1572872 | tf_op jit(solution)/shard_map/ppermute | solution.py:14
  111.1 49.1 %collective-permute-start.21 = (bf16[1024,256]{1,0:T(8,128)(2,1)S(1)}, bf16[1024,256]{1,0:T(8,128)(2,1)}, u32[]{:S(2)}, u32[]{:S(2)}) collective-permute-start(bf16[1024,256]{1,0:T(8,128)(2,1)S(1)} %get-tuple-element.123), channel_id=1, source_target_pairs={{0,2},{1,3},{2,0},{3,1},{4,6},{5,7},{6,4},{7,5},{8,10},{9,11},{10,... | collective-permute-start | bytes 1572872 | tf_op jit(solution)/shard_map/ppermute | solution.py:19
  163.3 52.6 %collective-permute-start.17 = (bf16[1024,256]{1,0:T(8,128)(2,1)}, bf16[1024,256]{1,0:T(8,128)(2,1)}, u32[]{:S(2)}, u32[]{:S(2)}) collective-permute-start(bf16[1024,256]{1,0:T(8,128)(2,1)} %slice.569), channel_id=1, source_target_pairs={{0,2},{1,3},{2,0},{3,1},{4,6},{5,7},{6,4},{7,5},{8,10},{9,11},{10,... | collective-permute-start | bytes 1572872 | tf_op jit(solution)/shard_map/ppermute | solution.py:19
  165.4 55.7 %collective-permute-start.28 = (bf16[1024,256]{1,0:T(8,128)(2,1)}, bf16[1024,256]{1,0:T(8,128)(2,1)}, u32[]{:S(2)}, u32[]{:S(2)}) collective-permute-start(bf16[1024,256]{1,0:T(8,128)(2,1)} %slice.566), channel_id=1, source_target_pairs={{0,2},{1,3},{2,0},{3,1},{4,6},{5,7},{6,4},{7,5},{8,10},{9,11},{10,... | collective-permute-start | bytes 1572872 | tf_op jit(solution)/shard_map/ppermute | solution.py:19
  196.1 76.7 %collective-permute-start.69 = (bf16[4,128,1152]{2,1,0:T(8,128)(2,1)S(1)}, bf16[4,128,1152]{2,1,0:T(8,128)(2,1)S(1)}, u32[]{:S(2)}, u32[]{:S(2)}) collective-permute-start(bf16[4,128,1152]{2,1,0:T(8,128)(2,1)S(1)} %fusion.40), channel_id=1, source_target_pairs={{0,4},{4,0},{8,12},{12,8},{16,20},{20,16},{24,28},{28,24},{1,5},{5... | collective-permute-start | bytes 3538952 | tf_op jit(solution)/shard_map/ppermute | solution.py:97
  223.9 38.6 %collective-permute-start.34 = (bf16[1024,256]{1,0:T(8,128)(2,1)S(1)}, bf16[1024,256]{1,0:T(8,128)(2,1)S(1)}, u32[]{:S(2)}, u32[]{:S(2)}) collective-permute-start(bf16[1024,256]{1,0:T(8,128)(2,1)S(1)} %get-tuple-element.77), channel_id=1, source_target_pairs={{0,2},{1,3},{2,0},{3,1},{4,6},{5,7},{6,4},{7,5},{8,10},{9,11},{10,... | collective-permute-start | bytes 1572872 | tf_op jit(solution)/shard_map/ppermute | solution.py:19
  225.2 35.6 %collective-permute-start.26 = (bf16[1024,256]{1,0:T(8,128)(2,1)S(1)}, bf16[1024,256]{1,0:T(8,128)(2,1)S(1)}, u32[]{:S(2)}, u32[]{:S(2)}) collective-permute-start(bf16[1024,256]{1,0:T(8,128)(2,1)S(1)} %slice.567), channel_id=1, source_target_pairs={{0,2},{1,3},{2,0},{3,1},{4,6},{5,7},{6,4},{7,5},{8,10},{9,11},{10,... | collective-permute-start | bytes 1572872 | tf_op jit(solution)/shard_map/ppermute | solution.py:19
  226.2 37.3 %collective-permute-start.37 = (bf16[1024,256]{1,0:T(8,128)(2,1)S(1)}, bf16[1024,256]{1,0:T(8,128)(2,1)S(1)}, u32[]{:S(2)}, u32[]{:S(2)}) collective-permute-start(bf16[1024,256]{1,0:T(8,128)(2,1)S(1)} %slice.565), channel_id=1, source_target_pairs={{0,2},{1,3},{2,0},{3,1},{4,6},{5,7},{6,4},{7,5},{8,10},{9,11},{10,... | collective-permute-start | bytes 1572872 | tf_op jit(solution)/shard_map/ppermute | solution.py:19
  227.6 33.2 %collective-permute-start.39 = (f32[1024]{0:T(1024)S(1)}, f32[1024]{0:T(1024)S(1)}, u32[]{:S(2)}, u32[]{:S(2)}) collective-permute-start(f32[1024]{0:T(1024)S(1)} %add.504), channel_id=1, source_target_pairs={{0,2},{1,3},{2,0},{3,1},{4,6},{5,7},{6,4},{7,5},{8,10},{9,11},{10,... | collective-permute-start | bytes 12296 | tf_op jit(solution)/shard_map/ppermute | solution.py:19
  260.8 28.8 %collective-permute-start.63 = (bf16[2,256,1152]{2,1,0:T(8,128)(2,1)S(1)}, bf16[2,256,1152]{2,1,0:T(8,128)(2,1)S(1)}, u32[]{:S(2)}, u32[]{:S(2)}) collective-permute-start(bf16[2,256,1152]{2,1,0:T(8,128)(2,1)S(1)} %fusion.39), channel_id=1, source_target_pairs={{0,8},{4,12},{8,0},{12,4},{16,24},{20,28},{24,16},{28,20},{1,9},{5... | collective-permute-start | bytes 3538952 | tf_op jit(solution)/shard_map/ppermute | solution.py:97
  262.5 29.3 %collective-permute-start.66 = (bf16[4,128,1152]{2,1,0:T(8,128)(2,1)S(1)}, bf16[4,128,1152]{2,1,0:T(8,128)(2,1)S(1)}, u32[]{:S(2)}, u32[]{:S(2)}) collective-permute-start(bf16[4,128,1152]{2,1,0:T(8,128)(2,1)S(1)} %fusion.38), channel_id=1, source_target_pairs={{0,4},{4,0},{8,12},{12,8},{16,20},{20,16},{24,28},{28,24},{1,5},{5... | collective-permute-start | bytes 3538952 | tf_op jit(solution)/shard_map/ppermute | solution.py:97
  265.3 27.0 %collective-permute-start.40 = (bf16[1024,256]{1,0:T(8,128)(2,1)S(1)}, bf16[1024,256]{1,0:T(8,128)(2,1)S(1)}, u32[]{:S(2)}, u32[]{:S(2)}) collective-permute-start(bf16[1024,256]{1,0:T(8,128)(2,1)S(1)} %get-tuple-element.81), channel_id=1, source_target_pairs={{0,1},{1,0},{2,3},{3,2},{4,5},{5,4},{6,7},{7,6},{8,9},{9,8},{10,11... | collective-permute-start | bytes 1572872 | tf_op jit(solution)/shard_map/ppermute | solution.py:14
  267.0 25.8 %collective-permute-start.41 = (bf16[1024,256]{1,0:T(8,128)(2,1)S(1)}, bf16[1024,256]{1,0:T(8,128)(2,1)S(1)}, u32[]{:S(2)}, u32[]{:S(2)}) collective-permute-start(bf16[1024,256]{1,0:T(8,128)(2,1)S(1)} %get-tuple-element.81), channel_id=1, source_target_pairs={{0,2},{1,3},{2,0},{3,1},{4,6},{5,7},{6,4},{7,5},{8,10},{9,11},{10,... | collective-permute-start | bytes 1572872 | tf_op jit(solution)/shard_map/ppermute | solution.py:19
  274.1 80.7 %collective-permute-start.70 = (bf16[2,128,1152]{2,1,0:T(8,128)(2,1)}, bf16[2,128,1152]{2,1,0:T(8,128)(2,1)}, u32[]{:S(2)}, u32[]{:S(2)}) collective-permute-start(bf16[2,128,1152]{2,1,0:T(8,128)(2,1)} %fusion.78), channel_id=1, source_target_pairs={{0,8},{4,12},{8,0},{12,4},{16,24},{20,28},{24,16},{28,20},{1,9},{5... | collective-permute-start | bytes 1769480 | tf_op jit(solution)/shard_map/ppermute | solution.py:97
  290.9 65.1 %collective-permute-start.64 = (bf16[2,128,1152]{2,1,0:T(8,128)(2,1)}, bf16[2,128,1152]{2,1,0:T(8,128)(2,1)}, u32[]{:S(2)}, u32[]{:S(2)}) collective-permute-start(bf16[2,128,1152]{2,1,0:T(8,128)(2,1)} %fusion.77), channel_id=1, source_target_pairs={{0,4},{4,0},{8,12},{12,8},{16,20},{20,16},{24,28},{28,24},{1,5},{5... | collective-permute-start | bytes 1769480 | tf_op jit(solution)/shard_map/ppermute | solution.py:97
  302.7 24.9 %collective-permute-start.57 = (f32[4,256]{1,0:T(4,128)S(1)}, f32[4,256]{1,0:T(4,128)S(1)}, u32[]{:S(2)}, u32[]{:S(2)}) collective-permute-start(f32[4,256]{1,0:T(4,128)S(1)} %pad_maximum_fusion.49), channel_id=1, source_target_pairs={{0,4},{4,0},{8,12},{12,8},{16,20},{20,16},{24,28},{28,24},{1,5},{5... | collective-permute-start | bytes 12296 | tf_op jit(solution)/shard_map/ppermute | solution.py:77
  339.8 21.6 %collective-permute-start.60 = (bf16[4,128,256]{2,1,0:T(8,128)(2,1)}, bf16[4,128,256]{2,1,0:T(8,128)(2,1)S(1)}, u32[]{:S(2)}, u32[]{:S(2)}) collective-permute-start(bf16[4,128,256]{2,1,0:T(8,128)(2,1)} %fusion.85), channel_id=1, source_target_pairs={{0,4},{4,0},{8,12},{12,8},{16,20},{20,16},{24,28},{28,24},{1,5},{5... | collective-permute-start | bytes 786440 | tf_op jit(solution)/shard_map/ppermute | solution.py:97
  352.6 53.0 %collective-permute-start.54 = (bf16[4,128,768]{2,1,0:T(8,128)(2,1)}, bf16[4,128,768]{2,1,0:T(8,128)(2,1)}, u32[]{:S(2)}, u32[]{:S(2)}) collective-permute-start(bf16[4,128,768]{2,1,0:T(8,128)(2,1)} %bitcast.332), channel_id=1, source_target_pairs={{0,4},{4,0},{8,12},{12,8},{16,20},{20,16},{24,28},{28,24},{1,5},{5... | collective-permute-start | bytes 2359304 | tf_op jit(solution)/shard_map/ppermute | solution.py:97
  354.8 54.7 %collective-permute-start.43 = (bf16[1024,512]{1,0:T(8,128)(2,1)}, bf16[1024,512]{1,0:T(8,128)(2,1)}, u32[]{:S(2)}, u32[]{:S(2)}) collective-permute-start(bf16[1024,512]{1,0:T(8,128)(2,1)} %bitcast_convert_fusion.4), channel_id=1, source_target_pairs={{0,1},{1,0},{2,3},{3,2},{4,5},{5,4},{6,7},{7,6},{8,9},{9,8},{10,11... | collective-permute-start | bytes 3145736 | tf_op jit(solution)/shard_map/ppermute | solution.py:14
  356.0 58.0 %collective-permute-start.47 = (bf16[1024,512]{1,0:T(8,128)(2,1)}, bf16[1024,512]{1,0:T(8,128)(2,1)}, u32[]{:S(2)}, u32[]{:S(2)}) collective-permute-start(bf16[1024,512]{1,0:T(8,128)(2,1)} %bitcast_convert_fusion.3), channel_id=1, source_target_pairs={{0,1},{1,0},{2,3},{3,2},{4,5},{5,4},{6,7},{7,6},{8,9},{9,8},{10,11... | collective-permute-start | bytes 3145736 | tf_op jit(solution)/shard_map/ppermute | solution.py:14
  357.9 23.8 %collective-permute-start.71 = (bf16[1,128,1152]{2,1,0:T(8,128)(2,1)S(1)}, bf16[1,128,1152]{2,1,0:T(8,128)(2,1)S(1)}, u32[]{:S(2)}, u32[]{:S(2)}) collective-permute-start(bf16[1,128,1152]{2,1,0:T(8,128)(2,1)S(1)} %dynamic-slice_convert_fusion.3), channel_id=1, source_target_pairs={{0,16},{4,20},{8,24},{12,28},{16,0},{20,4},{24,8},{28,12},{1,17},{... | collective-permute-start | bytes 884744 | tf_op jit(solution)/shard_map/ppermute | solution.py:97
  361.4 32.9 %collective-permute-start.65 = (bf16[1,128,1152]{2,1,0:T(8,128)(2,1)S(1)}, bf16[1,128,1152]{2,1,0:T(8,128)(2,1)S(1)}, u32[]{:S(2)}, u32[]{:S(2)}) collective-permute-start(bf16[1,128,1152]{2,1,0:T(8,128)(2,1)S(1)} %dynamic-slice_convert_fusion.5), channel_id=1, source_target_pairs={{0,16},{4,20},{8,24},{12,28},{16,0},{20,4},{24,8},{28,12},{1,17},{... | collective-permute-start | bytes 884744 | tf_op jit(solution)/shard_map/ppermute | solution.py:97
  412.9 21.5 %collective-permute-start.44 = (bf16[1024,256]{1,0:T(8,128)(2,1)}, bf16[1024,256]{1,0:T(8,128)(2,1)}, u32[]{:S(2)}, u32[]{:S(2)}) collective-permute-start(bf16[1024,256]{1,0:T(8,128)(2,1)} %slice.564), channel_id=1, source_target_pairs={{0,2},{1,3},{2,0},{3,1},{4,6},{5,7},{6,4},{7,5},{8,10},{9,11},{10,... | collective-permute-start | bytes 1572872 | tf_op jit(solution)/shard_map/ppermute | solution.py:19
  (157 other events, 1384.1 us)
